TPU v7x, 32 devices: a whole 2x2x4 slice. The times are simulated.
32 devices in a mesh: ctx: 8 (over y, x, core), wsh: 4 (over z).
Axes of the slice: x: 2, y: 2, z: 4, core: 2. Of those that a mesh axis runs over, the one named last changes fastest.
Arguments:
- hidden_state: bfloat16 [12, 2048, 512], P('wsh', 'ctx'), may hold values from -1.6953125 to 1.6953125
- prev_state: bfloat16 [12, 2048, 512], P('wsh', 'ctx'), may hold values from -1.6953125 to 1.6953125
- halt_sum: float32 [12, 2048], P('wsh', 'ctx'), may hold values from 0 to 0.9
- halt_code: int32 [12, 2048], P('wsh', 'ctx'), may hold values from 0 to 2
- step_count: int32 [12, 2048], P('wsh', 'ctx'), may hold values from 0 to 3
- w_query: bfloat16 [512, 512], P(None, 'wsh'), may hold values from -0.25 to 0.25
- w_key: bfloat16 [512, 512], P(None, 'wsh'), may hold values from -0.25 to 0.25
- w_value: bfloat16 [512, 512], P(None, 'wsh'), may hold values from -0.25 to 0.25
- w_out: bfloat16 [512, 512], P('wsh'), may hold values from -2.5 to 2.5
- w_inner: bfloat16 [512, 2048], P(None, 'wsh'), may hold values from -0.25 to 0.25
- b_inner: bfloat16 [2048], P('wsh'), may hold values from -2.5 to 2.5
- w_outer: bfloat16 [2048, 512], P('wsh'), may hold values from -0.125 to 0.125
- b_outer: bfloat16 [512], P('wsh'), may hold values from -2.5 to 2.5
- gain_attention: bfloat16 [512], P('wsh'), may hold values from 0.099609375 to 1.8984375
- shift_attention: bfloat16 [512], P('wsh'), may hold values from -2.5 to 2.5
- gain_feedforward: bfloat16 [512], P('wsh'), may hold values from 0.099609375 to 1.8984375
- shift_feedforward: bfloat16 [512], P('wsh'), may hold values from -2.5 to 2.5
- w_halt: bfloat16 [512], P('wsh'), may hold values from -0.25 to 0.25
- b_halt: float32 [1], replicated, may hold values from -1 to 1
- grad_transformed: bfloat16 [12, 2048, 512], P('wsh', 'ctx'), may hold values from -1.6953125 to 1.6953125
- grad_blended: bfloat16 [12, 2048, 512], P('wsh', 'ctx'), may hold values from -1.6953125 to 1.6953125
- grad_sum: float32 [12, 2048], P('wsh', 'ctx'), may hold values from -1.7 to 1.7
Outputs:
- transformed: bfloat16 [12, 2048, 512], P('wsh', 'ctx')
- blended: bfloat16 [12, 2048, 512], P('wsh', 'ctx')
- new_sum: float32 [12, 2048], P('wsh', 'ctx')
- grad_state: float32 [12, 2048, 512], P('wsh', 'ctx')
- grad_prev: float32 [12, 2048, 512], P('wsh', 'ctx')
- grad_halt_sum: float32 [12, 2048], P('wsh', 'ctx')
- grad_w_query: float32 [512, 512], P(None, 'wsh')
- grad_w_key: float32 [512, 512], P(None, 'wsh')
- grad_w_value: float32 [512, 512], P(None, 'wsh')
- grad_w_out: float32 [512, 512], P('wsh')
- grad_w_inner: float32 [512, 2048], P(None, 'wsh')
- grad_b_inner: float32 [2048], P('wsh')
- grad_w_outer: float32 [2048, 512], P('wsh')
- grad_b_outer: float32 [512], P('wsh')
- grad_gain_attention: float32 [512], P('wsh')
- grad_shift_attention: float32 [512], P('wsh')
- grad_gain_feedforward: float32 [512], P('wsh')
- grad_shift_feedforward: float32 [512], P('wsh')
- grad_w_halt: float32 [512], P('wsh')
- grad_b_halt: float32 [1], replicated
Inputs may be any that keep to these rules, and one draw needn't show every extreme that they name: halt_code is 0 for a token that halted earlier, 1 for one that keeps running, 2 for one that halts at this step.
All inputs are finite; a program needn't handle non-finite values.
Results may differ from a plain program's by a relative error of at most 0.028.
Values may be sent and summed in bfloat16 or wider, within the bound.
No kernel may reach another device: no remote copies, remote signals or barrier semaphores. Data moves between devices by JAX's collectives and lax.ppermute only.
A program may use at most 320 MiB of HBM per device.

v0:
```python
import functools
import math

import jax
import jax.numpy as jnp
from jax import lax
from jax.experimental import pallas as pl
from jax.experimental.pallas import tpu as pltpu
from jax.sharding import PartitionSpec as P

HEADS = 8
PAIRS = 4
WIDE = 128
SMALL = 16
epsilon = 1e-06
f32 = jnp.float32
bf16 = jnp.bfloat16
LOG2E = math.log2(math.e)
NT = (((1,), (1,)), ((), ()))
TN = (((0,), (0,)), ((), ()))
NN = (((1,), (0,)), ((), ()))
MIB = 1024 * 1024
KEYS = 256


def room(mebibytes):
    return pltpu.CompilerParams(vmem_limit_bytes=int(mebibytes) * MIB)


def cost(micros):
    return pl.CostEstimate(flops=int(micros * 1.1e9), bytes_accessed=1024, transcendentals=0)


def dot(a, b, dims=NN):
    return lax.dot_general(a, b, dims, preferred_element_type=f32)


def lane_masks(shape):
    lane = lax.broadcasted_iota(jnp.int32, shape, 1)
    return lane < WIDE // 2


def largest_squares(refs):
    same = (
        lax.broadcasted_iota(jnp.int32, (WIDE, WIDE), 0) // (WIDE // 2)
        == lax.broadcasted_iota(jnp.int32, (WIDE, WIDE), 1) // (WIDE // 2)
    ).astype(bf16)
    most = None
    for ref in refs:
        for start in range(0, ref.shape[1], 1024):
            x = ref[0, start : start + 1024, :WIDE].astype(f32)
            top = jnp.max(dot((x * x).astype(bf16), same), axis=0, keepdims=True)
            most = top if most is None else jnp.maximum(most, top)
    return most


def attend_kernel(blocks, carried, q_ref, *refs):
    kv_refs = refs[:blocks]
    refs = refs[blocks + carried :]
    flag_ref = refs[-1]
    o_ref, mass_ref, low_refs = refs[0], refs[1], refs[2:-1]
    scale = 0.125 * LOG2E
    index = pl.program_id(0)
    step = o_ref.shape[1]

    @pl.when(index == 0)
    def _():
        bound = jnp.max(largest_squares([q_ref]) * largest_squares(kv_refs))
        flag_ref[0] = (bound < 0.98 * (8.0 * 70.0) ** 2).astype(jnp.int32)

    q = q_ref[0, pl.ds(pl.multiple_of(index * step, step), step)]
    first = lane_masks(q.shape)
    none = jnp.zeros_like(q)
    size = KEYS
    chunks = [(ref, start) for ref in kv_refs for start in range(0, ref.shape[1], size)]

    def finish(outs, masses):
        out = jnp.where(first, outs[0], outs[1])
        o_ref[0] = out
        low = out.astype(bf16)
        block = low_refs[0].shape[1]
        for d, ref in enumerate(low_refs):

            @pl.when(index == d * block // step)
            def _(ref=ref, at=d * block % step):
                ref[0] = low[at : at + block]

        table = jnp.where(first, masses[0], masses[1])
        turned = jnp.transpose(table)
        mass_ref[0] = jnp.concatenate([turned[0:4], turned[64:68]], axis=0)

    def masked(head):
        return jnp.where(first, q, none) if head == 0 else jnp.where(first, none, q)

    def lanes(e):
        return sum(e[:, i : i + 128] for i in range(0, size, 128))

    @pl.when(flag_ref[0] == 1)
    def _():
        outs, masses = [], []
        for head in range(2):
            mine = masked(head)
            total = None
            weighted = None
            for ref, start in chunks:
                e = jnp.exp2(dot(mine, ref[0, start : start + size, :WIDE], NT) * scale)
                w = dot(e.astype(bf16), ref[0, start : start + size, WIDE:])
                total = lanes(e) if total is None else total + lanes(e)
                weighted = w if weighted is None else weighted + w
            total = jnp.sum(total, axis=1, keepdims=True)
            outs.append(weighted * (1.0 / total))
            masses.append(jnp.log2(total))
        finish(outs, masses)

    @pl.when(flag_ref[0] != 1)
    def _():
        outs, masses = [], []
        for head in range(2):
            mine = masked(head)
            fold = (
                jnp.zeros((step, WIDE), f32),
                jnp.full((step, 1), -jnp.inf, f32),
                jnp.zeros((step, 1), f32),
            )
            for ref in kv_refs:

                def body(i, fold, ref=ref, mine=mine):
                    weighted, top, total = fold
                    at = pl.ds(pl.multiple_of(i * size, size), size)
                    scores = dot(mine, ref[0, at, :WIDE], NT) * scale
                    now = jnp.maximum(top, jnp.max(scores, axis=1, keepdims=True))
                    factor = jnp.exp2(top - now)
                    e = jnp.exp2(scores - now)
                    total = total * factor + jnp.sum(e, axis=1, keepdims=True)
                    weighted = weighted * factor + dot(e.astype(bf16), ref[0, at, WIDE:])
                    return weighted, now, total

                fold = lax.fori_loop(0, ref.shape[1] // size, body, fold)
            weighted, top, total = fold
            outs.append(weighted * (1.0 / total))
            masses.append(top + jnp.log2(total))
        finish(outs, masses)


def attend(at, seqs, q, kvs, before):
    _, rows, _ = q.shape
    block = rows // PAIRS
    keys = sum(kv.shape[1] for kv in kvs)
    step = 2 * block if keys <= 2048 else block
    shapes = [
        jax.ShapeDtypeStruct((seqs, rows, WIDE), f32),
        jax.ShapeDtypeStruct((seqs, 8, rows), f32),
    ] + [jax.ShapeDtypeStruct((seqs, block, WIDE), bf16)] * PAIRS
    carried = len(shapes) if before else 0
    return pl.pallas_call(
        functools.partial(attend_kernel, len(kvs), carried),
        grid=(rows // step,),
        in_specs=[full_spec(q)]
        + [full_spec(kv) for kv in kvs]
        + [pl.BlockSpec(memory_space=pl.ANY)] * carried,
        out_specs=[
            pl.BlockSpec((1, step, WIDE), lambda i: (at, i, 0)),
            pl.BlockSpec((1, 8, step), lambda i: (at, 0, i)),
        ]
        + [pl.BlockSpec((1, block, WIDE), lambda i: (at, 0, 0))] * PAIRS,
        out_shape=shapes,
        input_output_aliases={1 + len(kvs) + i: i for i in range(carried)},
        scratch_shapes=[pltpu.SMEM((1,), jnp.int32)],
        compiler_params=room(24 if keys <= 2048 else 10 + keys // 256),
        cost_estimate=cost(1),
        name="attend",
    )(q, *kvs, *(before or ()))


def attend_back_kernel(blocks, q_ref, *refs):
    g_refs, o_ref, mass_ref = refs[:PAIRS], refs[PAIRS], refs[PAIRS + 1]
    refs = refs[PAIRS + 2 :]
    kv_refs = refs[:blocks]
    dq_ref = refs[blocks]
    dkv_refs = refs[blocks + 1 : 2 * blocks + 1]
    dq_acc = refs[2 * blocks + 1]
    scale = 0.125 * LOG2E
    q = q_ref[0]
    g = jnp.concatenate([ref[0] for ref in g_refs], axis=0)
    first = lane_masks(q.shape)
    none = jnp.zeros_like(q)
    qs = [jnp.where(first, q, none), jnp.where(first, none, q)]
    gs = [jnp.where(first, g, none), jnp.where(first, none, g)]
    product = g.astype(f32) * o_ref[0]
    which = lax.broadcasted_iota(jnp.int32, (8, WIDE), 0) == (
        lax.broadcasted_iota(jnp.int32, (8, WIDE), 1) // (WIDE // 2)
    )
    deltas = lax.dot_general(
        which.astype(f32), product, NT, precision=lax.Precision.HIGHEST, preferred_element_type=f32
    )
    delta = [deltas[0:1], deltas[1:2]]
    mass = [mass_ref[0, 0:1, :], mass_ref[0, 4:5, :]]
    dq_acc[...] = jnp.zeros_like(dq_acc)
    size = 256
    key_first = lane_masks((size, WIDE))
    key_none = jnp.zeros((size, WIDE), bf16)

    for kv_ref, dkv_ref in zip(kv_refs, dkv_refs):

        def chunk(i, carry, kv_ref=kv_ref, dkv_ref=dkv_ref):
            at = pl.ds(pl.multiple_of(i * size, size), size)
            k = kv_ref[0, at, :WIDE]
            v = kv_ref[0, at, WIDE:]
            dk = dv = dq = None
            for head in range(2):
                s = dot(k, qs[head], NT)
                p = jnp.exp2(s * scale - mass[head])
                dp = dot(v, gs[head], NT)
                ds = (p * (dp - delta[head])).astype(bf16)
                own_v = dot(p.astype(bf16), gs[head])
                own_k = dot(ds, qs[head])
                km = jnp.where(key_first, k, key_none) if head == 0 else jnp.where(key_first, key_none, k)
                own_q = dot(ds, km, TN)
                dv = own_v if dv is None else dv + own_v
                dk = own_k if dk is None else dk + own_k
                dq = own_q if dq is None else dq + own_q
            dkv_ref[0, at, :WIDE] = (dk * 0.125).astype(dkv_ref.dtype)
            dkv_ref[0, at, WIDE:] = dv.astype(dkv_ref.dtype)
            dq_acc[...] += dq
            return carry

        lax.fori_loop(0, kv_ref.shape[1] // size, chunk, 0, unroll=2)
    dq_ref[0] = (dq_acc[...] * 0.125).astype(bf16)


def attend_back(at, q, gs, o, mass, kvs, kinds):
    _, rows, _ = q.shape
    keys = sum(kv.shape[1] for kv in kvs)
    own = gs[0].shape[1]
    whole = lambda width: pl.BlockSpec((1, rows, width), lambda s: (0, 0, 0))
    kv_specs = [pl.BlockSpec((1, kv.shape[1], 2 * WIDE), lambda s: (0, 0, 0)) for kv in kvs]
    return pl.pallas_call(
        functools.partial(attend_back_kernel, len(kvs)),
        grid=(1,),
        in_specs=[whole(WIDE)]
        + [pl.BlockSpec((1, own, WIDE), lambda s: (at, 0, 0))] * PAIRS
        + [pl.BlockSpec((1, rows, WIDE), lambda s: (at, 0, 0)), pl.BlockSpec((1, 8, rows), lambda s: (at, 0, 0))]
        + kv_specs,
        out_specs=[whole(WIDE)] + kv_specs,
        out_shape=[jax.ShapeDtypeStruct((1, rows, WIDE), bf16)]
        + [jax.ShapeDtypeStruct(kv.shape, kind) for kv, kind in zip(kvs, kinds)],
        scratch_shapes=[pltpu.VMEM((rows, WIDE), f32)],
        compiler_params=room(14 + keys // 512),
        cost_estimate=cost(14),
        name="attend_back",
    )(q, *gs, o, mass, *kvs)


def full_spec(array):
    return pl.BlockSpec(array.shape, lambda *_: (0,) * array.ndim)


def pack_kernel(info_ref, *refs):
    parts, out_ref = refs[:-1], refs[-1]
    core = info_ref[0]
    half = out_ref.shape[0]

    @pl.when(core == 0)
    def _():
        out_ref[...] = jnp.concatenate([ref[:half] for ref in parts], axis=1)

    @pl.when(core != 0)
    def _():
        out_ref[...] = jnp.concatenate([ref[half:] for ref in parts], axis=1)


def pack(info, parts):
    rows, width = parts[0].shape
    shape = (rows // 2, len(parts) * width)
    return pl.pallas_call(
        pack_kernel,
        grid=(1,),
        in_specs=[pl.BlockSpec(memory_space=pltpu.SMEM)] + [full_spec(x) for x in parts],
        out_specs=pl.BlockSpec(shape, lambda i: (0, 0)),
        out_shape=jax.ShapeDtypeStruct(shape, bf16),
        compiler_params=room(6),
        cost_estimate=cost(1),
        name="pack",
    )(info, *parts)


def pack_feed_kernel(info_ref, inner_ref, outer_ref, wout_ref, bias_ref, *refs):
    vectors, out_ref = refs[:-1], refs[-1]
    core = info_ref[0]
    width = inner_ref.shape[0]
    cut = wout_ref.shape[0] // 2

    @pl.when(core == 0)
    def _():
        out_ref[:width] = inner_ref[...]
        out_ref[width : width + cut] = wout_ref[:cut]

    @pl.when(core != 0)
    def _():
        out_ref[:width] = outer_ref[...]
        out_ref[width : width + cut] = wout_ref[cut:]

    row = lax.broadcasted_iota(jnp.int32, (SMALL, WIDE), 0)
    table = jnp.zeros((SMALL, WIDE), f32)
    for i, ref in enumerate(vectors):
        table = jnp.where(row == i + 1, ref[...].astype(f32), table)
    row = lax.broadcasted_iota(jnp.int32, (SMALL, width), 0)
    table = jnp.concatenate([table, jnp.zeros((SMALL, width - WIDE), f32)], axis=1)
    table = jnp.where(row == 0, bias_ref[...].astype(f32), table)
    out_ref[width + cut :] = table.astype(bf16)


def pack_feed(info, w_inner, w_outer, w_out, b_inner, vectors):
    width = w_inner.shape[0]
    parts = [w_inner, w_outer, w_out, b_inner.reshape(1, -1)] + [v.reshape(1, -1) for v in vectors]
    shape = (width + w_out.shape[0] // 2 + SMALL, w_out.shape[1])
    return pl.pallas_call(
        pack_feed_kernel,
        grid=(1,),
        in_specs=[pl.BlockSpec(memory_space=pltpu.SMEM)] + [full_spec(x) for x in parts],
        out_specs=pl.BlockSpec(shape, lambda i: (0, 0)),
        out_shape=jax.ShapeDtypeStruct(shape, bf16),
        compiler_params=room(10),
        cost_estimate=cost(2),
        name="pack_feed",
    )(info, *parts)


def project_kernel(count, *refs):
    blocks, w_ref, q_ref, kv_ref = refs[:count], refs[count], refs[count + 1], refs[count + 2]
    at = 0
    for ref in blocks:
        rows = ref.shape[1]
        made = dot(ref[0], w_ref[...]).astype(bf16)
        q_ref[0, at : at + rows] = made[:, :WIDE]
        kv_ref[0, at : at + rows] = made[:, WIDE:]
        at += rows


def project(at, tokens, w_mine):
    total = sum(x.shape[1] for x in tokens)
    return pl.pallas_call(
        functools.partial(project_kernel, len(tokens)),
        grid=(1,),
        in_specs=[pl.BlockSpec((1,) + x.shape[1:], lambda i: (at, 0, 0)) for x in tokens]
        + [full_spec(w_mine)],
        out_specs=[
            pl.BlockSpec((1, total, WIDE), lambda i: (0, 0, 0)),
            pl.BlockSpec((1, total, 2 * WIDE), lambda i: (0, 0, 0)),
        ],
        out_shape=[
            jax.ShapeDtypeStruct((1, total, WIDE), bf16),
            jax.ShapeDtypeStruct((1, total, 2 * WIDE), bf16),
        ],
        compiler_params=room(10),
        cost_estimate=cost(1),
        name="project",
    )(*tokens, w_mine)


def combine_kernel(chosen, count, prior, final, info_ref, *refs):
    blocks, refs = refs[:count], refs[count:]
    backs, refs = refs[: 3 * len(chosen)], refs[3 * len(chosen) :]
    grad = None
    if prior:
        grad, refs = refs[0][...], refs[1:]
    outs, grad_refs = refs[:PAIRS], refs[PAIRS:]
    rows = outs[0].shape[1]
    for i, s in enumerate(chosen):
        dq_ref, kept_ref, got_ref = backs[3 * i : 3 * i + 3]
        at = 0
        for ref in blocks:
            size = ref.shape[1]
            part = slice(at, at + size)
            dkv = (kept_ref[0, part] + got_ref[0, part].astype(f32)).astype(bf16)
            piece = jnp.concatenate([dq_ref[0, part], dkv], axis=1)
            outs[at // rows][i, at % rows : at % rows + size] = piece
            term = dot(ref[s], piece, TN)
            grad = term if grad is None else grad + term
            at += size
    if not final:
        grad_refs[0][...] = grad
        return
    size = grad.shape[0] // (2 * PAIRS)

    def write(even_ref, odd_ref):
        for c in range(2 * PAIRS):
            ref = even_ref if c % 2 == 0 else odd_ref
            ref[jnp.bitwise_xor(c // 2, info_ref[2])] = grad[c * size : (c + 1) * size].astype(ref.dtype)

    @pl.when(info_ref[0] == 0)
    def _():
        write(grad_refs[0], grad_refs[1])

    @pl.when(info_ref[0] != 0)
    def _():
        write(grad_refs[1], grad_refs[0])


def combine(info, chosen, tokens, backs, prior, final):
    _, rows, width = tokens[0].shape
    flat = [x for back in backs for x in back]
    extra = [] if prior is None else [prior]
    if final:
        shape = (PAIRS, width // (2 * PAIRS), 3 * WIDE)
        grads = [jax.ShapeDtypeStruct(shape, f32), jax.ShapeDtypeStruct(shape, bf16)]
    else:
        grads = [jax.ShapeDtypeStruct((width, 3 * WIDE), f32)]
    pieces = [jax.ShapeDtypeStruct((len(chosen), rows, 3 * WIDE), bf16)] * PAIRS
    return pl.pallas_call(
        functools.partial(combine_kernel, chosen, len(tokens), len(extra), final),
        grid=(1,),
        in_specs=[pl.BlockSpec(memory_space=pltpu.SMEM)] + [full_spec(x) for x in tokens + flat + extra],
        out_specs=[full_spec(x) for x in pieces + grads],
        out_shape=pieces + grads,
        compiler_params=room(20),
        cost_estimate=cost(2),
        name="combine",
    )(info, *tokens, *flat, *extra)


def join_small_kernel(keep_ref, got_ref, *outs):
    for d, out in enumerate(outs):
        out[...] = (keep_ref[d] + got_ref[d].astype(f32)).astype(bf16)


def join_small(keep, got):
    return pl.pallas_call(
        join_small_kernel,
        grid=(1,),
        in_specs=[full_spec(keep), full_spec(got)],
        out_specs=[pl.BlockSpec(keep.shape[1:], lambda i: (0, 0))] * PAIRS,
        out_shape=[jax.ShapeDtypeStruct(keep.shape[1:], bf16)] * PAIRS,
        compiler_params=room(6),
        cost_estimate=cost(1),
        name="join_small",
    )(keep, got)


def pack_heads(total):
    kept = total.shape[0] * 3 // 4
    rest = [total[kept:, i * WIDE : (i + 1) * WIDE] for i in range(3)]
    return jnp.concatenate([total[:kept], jnp.concatenate(rest, axis=0)], axis=1)


def share_small_kernel(info_ref, feed_ref, *refs):
    parts, outs = refs[:PAIRS], refs[PAIRS:]
    for step, out in enumerate(outs):
        at = jnp.bitwise_xor(jnp.bitwise_xor(info_ref[1], info_ref[2]), step)
        value = parts[0][...]
        for d in range(1, PAIRS):
            value = jnp.where(at == d, parts[d][...], value)
        value = pack_heads(value)
        if step == 2:
            rows = feed_ref.shape[0]
            out[:rows] = feed_ref[...]
            out[rows:] = value
        else:
            out[...] = value


def share_small(info, feed, parts):
    small = (parts[0].shape[0] * 3 // 4, feed.shape[1])
    large = (small[0] + feed.shape[0], feed.shape[1])
    shapes = [small, small, large, small]
    return pl.pallas_call(
        share_small_kernel,
        grid=(1,),
        in_specs=[pl.BlockSpec(memory_space=pltpu.SMEM)] + [full_spec(x) for x in [feed] + parts],
        out_specs=[pl.BlockSpec(shape, lambda i: (0, 0)) for shape in shapes],
        out_shape=[jax.ShapeDtypeStruct(shape, bf16) for shape in shapes],
        compiler_params=room(6),
        cost_estimate=cost(1),
        name="share_small",
    )(info, feed, *parts)


def state_kernel(base_ref, *refs):
    blocks, weights, out_ref = refs[:PAIRS], refs[PAIRS : 2 * PAIRS], refs[2 * PAIRS]
    total = base_ref[0]
    for ref, w_ref in zip(blocks, weights):
        total = total + dot(ref[0], w_ref[...], NT)
    out_ref[0] = total


def add_state(at, base, blocks, weights):
    rows, width = base.shape[1:]
    count = blocks[0].shape[0]
    spec = pl.BlockSpec((1, rows, width), lambda i: (at + i, 0, 0))
    return pl.pallas_call(
        state_kernel,
        grid=(count,),
        in_specs=[spec]
        + [pl.BlockSpec((1,) + b.shape[1:], lambda i: (i, 0, 0)) for b in blocks]
        + [full_spec(w) for w in weights],
        out_specs=spec,
        out_shape=jax.ShapeDtypeStruct(base.shape, base.dtype),
        input_output_aliases={0: 0},
        compiler_params=room(10),
        cost_estimate=cost(2.5 * count),
        name="add_state",
    )(base, *blocks, *weights)


def choose_kernel(info_ref, near_ref, far_ref, out_ref):
    close = jnp.bitwise_xor(info_ref[1], info_ref[2]) < 2
    out_ref[...] = jnp.where(close, near_ref[...], far_ref[...])


def choose(info, near, far):
    return pl.pallas_call(
        choose_kernel,
        grid=(1,),
        in_specs=[pl.BlockSpec(memory_space=pltpu.SMEM), full_spec(near), full_spec(far)],
        out_specs=full_spec(near),
        out_shape=jax.ShapeDtypeStruct(near.shape, bf16),
        compiler_params=room(6),
        cost_estimate=cost(1),
        name="choose",
    )(info, near, far)


def assemble_kernel(info_ref, mine_ref, other_ref, out_ref):
    half = mine_ref.shape[0]
    out_ref[:half] = jnp.where(info_ref[0] == 0, mine_ref[...], other_ref[...])
    out_ref[half:] = jnp.where(info_ref[0] == 0, other_ref[...], mine_ref[...])


def assemble(info, mine, other):
    shape = (2 * mine.shape[0], mine.shape[1])
    return pl.pallas_call(
        assemble_kernel,
        grid=(1,),
        in_specs=[pl.BlockSpec(memory_space=pltpu.SMEM), full_spec(mine), full_spec(other)],
        out_specs=pl.BlockSpec(shape, lambda i: (0, 0)),
        out_shape=jax.ShapeDtypeStruct(shape, bf16),
        compiler_params=room(6),
        cost_estimate=cost(1),
        name="assemble",
    )(info, mine, other)


def keep_scalar(block):
    tail = block[-8:]
    total = tail[:, :WIDE] + tail[:, WIDE : 2 * WIDE]
    high = total.astype(bf16).astype(f32)
    split = jnp.concatenate([high, total - high, tail[:, 2 * WIDE :]], axis=1)
    row = lax.broadcasted_iota(jnp.int32, tail.shape, 0)
    tail = jnp.where(row == 6, split, tail)
    return tail if block.shape[0] == 8 else jnp.concatenate([block[:-8], tail], axis=0)


def flat_rows(ref):
    return ref[...].reshape(-1, ref.shape[-1])


def write_pieces(info_ref, even_ref, odd_ref, grads, small):
    pieces = 2 * PAIRS * even_ref.shape[1]

    def write(keep_ref, give_ref):
        for c in range(pieces):
            ref = keep_ref if c % 2 == 0 else give_ref
            order = jnp.bitwise_xor((c // 2) % PAIRS, info_ref[2])
            repeat = c // (2 * PAIRS)
            at = 0
            for grad in grads:
                size = grad.shape[0] // pieces
                ref[order, repeat, 0, at : at + size] = grad[c * size : (c + 1) * size]
                at += size
            if small is not None:
                ref[order, repeat, 0, at : at + 8] = small if c == 0 else jnp.zeros_like(small)

    @pl.when(info_ref[0] == 0)
    def _():
        write(even_ref, odd_ref)

    @pl.when(info_ref[0] != 0)
    def _():
        write(odd_ref, even_ref)


def outer_grad_kernel(
    info_ref, a0_ref, a1_ref, a2_ref, a3_ref, ilow_ref, gfeed_ref, gbranch_ref, even_ref, odd_ref
):
    g_outer = dot(flat_rows(ilow_ref), flat_rows(gfeed_ref), TN).astype(bf16)
    order = jnp.bitwise_xor(pl.program_id(0), info_ref[2])
    low, high = order % 2 == 0, order < 2
    att = jnp.where(
        high,
        jnp.where(low, flat_rows(a0_ref), flat_rows(a1_ref)),
        jnp.where(low, flat_rows(a2_ref), flat_rows(a3_ref)),
    )
    g_out = dot(att, flat_rows(gbranch_ref), TN).astype(bf16)
    write_pieces(info_ref, even_ref, odd_ref, (g_outer, g_out), None)


def inner_grad_kernel(info_ref, nlow_ref, gin_ref, vsum_ref, bsum_ref, even_ref, odd_ref):
    g_in = dot(flat_rows(nlow_ref), flat_rows(gin_ref), TN).astype(bf16)
    vectors = sum(vsum_ref[s] for s in range(vsum_ref.shape[0]))
    bias = sum(bsum_ref[s] for s in range(bsum_ref.shape[0]))
    width = g_in.shape[1]
    low = jnp.concatenate([vectors, jnp.zeros((8, width - WIDE), f32)], axis=1)
    row = lax.broadcasted_iota(jnp.int32, (8, width), 0)
    small = keep_scalar(jnp.where(row == 7, bias, low)).astype(bf16)
    write_pieces(info_ref, even_ref, odd_ref, (g_in,), small)


def split_grads(kernel, name, info, arrays, specs, piece, width, ctx):
    shape = (PAIRS, ctx // (2 * PAIRS), PAIRS, piece, width)
    out_spec = pl.BlockSpec(shape[:2] + (1, piece, width), lambda z, info: (0, 0, z, 0, 0))
    return pl.pallas_call(
        kernel,
        grid_spec=pltpu.PrefetchScalarGridSpec(
            num_scalar_prefetch=1, grid=(PAIRS,), in_specs=specs, out_specs=[out_spec, out_spec]
        ),
        out_shape=[jax.ShapeDtypeStruct(shape, bf16)] * 2,
        compiler_params=room(24),
        cost_estimate=cost(4.5),
        name=name,
    )(info, *arrays)


def hidden_spec(array):
    seqs, rows, hidden = array.shape
    return pl.BlockSpec(
        (seqs, rows, hidden // PAIRS), lambda z, info: (0, 0, lax.rem(z - info[1] + PAIRS, PAIRS))
    )


def outer_grads(info, att, ilow, gfeed, gbranch, ctx):
    width = gfeed.shape[2]
    piece = (ilow.shape[2] // PAIRS + width // PAIRS) // ctx
    arrays = [*att, ilow, gfeed, gbranch]
    specs = [full_spec(x) for x in arrays]
    specs[PAIRS] = hidden_spec(ilow)
    return split_grads(outer_grad_kernel, "outer_grads", info, arrays, specs, piece, width, ctx)


def inner_grads(info, nlow, gin, vsum, bsum, ctx):
    width = nlow.shape[2]
    seqs = vsum.shape[0]
    specs = [
        full_spec(nlow),
        hidden_spec(gin),
        pl.BlockSpec((seqs, 8, WIDE), lambda z, info: (0, 0, z)),
        hidden_spec(bsum),
    ]
    piece = width // ctx + 8
    return split_grads(
        inner_grad_kernel, "inner_grads", info, [nlow, gin, vsum, bsum], specs, piece, gin.shape[2] // PAIRS, ctx
    )


def join_kernel(scalar, keep_ref, got_ref, *outs):
    for d, out in enumerate(outs):
        for r in range(out.shape[0]):
            total = keep_ref[d, r, 0].astype(f32) + got_ref[d, r, 0].astype(f32)
            out[r, 0] = (keep_scalar(total) if scalar else total).astype(bf16)


def join(keep, got, scalar):
    _, repeats, wsh, piece, width = keep.shape
    spec = pl.BlockSpec((PAIRS, repeats, 1, piece, width), lambda z: (0, 0, z, 0, 0))
    return pl.pallas_call(
        functools.partial(join_kernel, scalar),
        grid=(wsh,),
        in_specs=[spec, spec],
        out_specs=[pl.BlockSpec((repeats, 1, piece, width), lambda z: (0, z, 0, 0))] * PAIRS,
        out_shape=[jax.ShapeDtypeStruct(keep.shape[1:], bf16)] * PAIRS,
        compiler_params=room(16),
        cost_estimate=cost(1.5),
        name="join",
    )(keep, got)


def share_kernel(info_ref, *refs):
    firsts, seconds, outs = refs[:PAIRS], refs[PAIRS : 2 * PAIRS], refs[2 * PAIRS :]
    for step in range(PAIRS):
        place = jnp.bitwise_xor(info_ref[1], step)
        out = outs[step % 2]
        for r in range(out.shape[0]):
            totals = []
            for parts in (firsts, seconds):
                total = parts[0][r, place].astype(f32)
                for part in parts[1:]:
                    total = total + part[r, place].astype(f32)
                totals.append(total)
            size = totals[0].shape[0]
            out[r, step // 2, :size] = totals[0].astype(bf16)
            out[r, step // 2, size:] = keep_scalar(totals[1]).astype(bf16)


def share_parts(info, firsts, seconds):
    repeats, wsh, piece, width = firsts[0].shape
    shape = (repeats, wsh // 2, piece + seconds[0].shape[2], width)
    return pl.pallas_call(
        share_kernel,
        grid=(1,),
        in_specs=[pl.BlockSpec(memory_space=pltpu.SMEM)] + [full_spec(x) for x in firsts + seconds],
        out_specs=[pl.BlockSpec(shape, lambda i: (0, 0, 0, 0))] * 2,
        out_shape=[jax.ShapeDtypeStruct(shape, bf16)] * 2,
        compiler_params=room(16),
        cost_estimate=cost(1.5),
        name="share",
    )(info, *firsts, *seconds)


def halve_kernel(keep_ref, got_ref, own_ref, send_ref):
    for at, out in enumerate((own_ref, send_ref)):
        out[...] = keep_scalar(keep_ref[at].astype(f32) + got_ref[at].astype(f32)).astype(bf16)


def halve(keep, got):
    shape = keep.shape[1:]
    return pl.pallas_call(
        halve_kernel,
        grid=(1,),
        in_specs=[full_spec(keep), full_spec(got)],
        out_specs=[pl.BlockSpec(shape, lambda i: (0, 0))] * 2,
        out_shape=[jax.ShapeDtypeStruct(shape, bf16)] * 2,
        compiler_params=room(6),
        cost_estimate=cost(1),
        name="halve",
    )(keep, got)


def total_kernel(own_ref, *refs):
    parts, out = refs[:-1], refs[-1]
    rows = own_ref.shape[0]
    if len(parts) == 1:
        out[...] = keep_scalar(own_ref[...].astype(f32) + parts[0][...].astype(f32)).astype(bf16)
        return
    out[:rows] = keep_scalar(own_ref[...].astype(f32) + parts[2][:rows].astype(f32)).astype(bf16)
    total = parts[2][rows:].astype(f32)
    for i in (0, 1, 3):
        total = total + parts[i][...].astype(f32)
    out[rows:] = total.astype(bf16)


def total_parts(own, parts):
    shape = max((x.shape for x in parts), key=lambda x: x[0])
    return pl.pallas_call(
        total_kernel,
        grid=(1,),
        in_specs=[full_spec(x) for x in [own] + parts],
        out_specs=pl.BlockSpec(shape, lambda i: (0, 0)),
        out_shape=jax.ShapeDtypeStruct(shape, bf16),
        compiler_params=room(6),
        cost_estimate=cost(1),
        name="total",
    )(own, *parts)


def unpack_kernel(info_ref, *refs):
    pieces = refs[: 2 * PAIRS]
    outer_ref, out_ref, in_ref, tail_ref, *heads = refs[2 * PAIRS :]
    core, pair = info_ref[0], info_ref[2]
    for side in range(2):
        for d in range(PAIRS):
            ref = pieces[side * PAIRS + d]
            place = jnp.bitwise_xor(pair, d) * 2 + jnp.bitwise_xor(core, side)
            at = 0
            for target in (outer_ref, out_ref, in_ref):
                size = target.shape[0] // (2 * PAIRS)
                start = pl.multiple_of(place * size, size)
                target[pl.ds(start, size)] = ref[at : at + size].astype(f32)
                at += size

            @pl.when(place == 0)
            def _(ref=ref, at=at):
                tail_ref[...] = ref[at : at + 8].astype(f32)

            at += 8
            size = heads[0].shape[0] // (2 * PAIRS)
            kept = size * 3 // 4
            for i, target in enumerate(heads):
                start = pl.multiple_of(place * size, size)
                target[pl.ds(start, kept)] = ref[at : at + kept, i * WIDE : (i + 1) * WIDE].astype(f32)
                more = (size - kept) * i + at
                target[pl.ds(start + kept, size - kept)] = ref[more : more + size - kept, 3 * WIDE :].astype(f32)


def unpack(info, mine, other, part, out_rows):
    width = mine[0].shape[1]
    shapes = [(part, width), (out_rows, width), (width, part), (8, width)] + [(width, WIDE)] * 3
    return pl.pallas_call(
        unpack_kernel,
        grid=(1,),
        in_specs=[pl.BlockSpec(memory_space=pltpu.SMEM)] + [full_spec(x) for x in mine + other],
        out_specs=[pl.BlockSpec(shape, lambda i: (0, 0)) for shape in shapes],
        out_shape=[jax.ShapeDtypeStruct(shape, f32) for shape in shapes],
        compiler_params=room(16),
        cost_estimate=cost(3),
        name="unpack",
    )(info, *mine, *other)


def gelu_parts(x):
    half = 0.5 * (1.0 + lax.erf(x * 2.0 ** (-0.5)))
    density = jnp.exp(-0.5 * x * x) * (2.0 * math.pi) ** (-0.5)
    return x * half, half + x * density


def mean_rows(x):
    return jnp.sum(x, axis=1, keepdims=True) * (1.0 / x.shape[1])


def norm_rows(z, gain, shift):
    centre = z - mean_rows(z)
    inverse = lax.rsqrt(mean_rows(centre * centre) + epsilon)
    normed = centre * inverse
    return normed * gain + shift, normed, inverse


def norm_back(g, normed, inverse, gain):
    scaled = g * gain
    return inverse * (scaled - mean_rows(scaled) - normed * mean_rows(scaled * normed))


def dense_kernel(info_ref, bhalt_ref, *refs):
    mine, other, refs = refs[:PAIRS], refs[PAIRS : 2 * PAIRS], refs[2 * PAIRS :]
    att_refs, refs = refs[:PAIRS], refs[PAIRS:]
    emb_ref, prev_ref, gt_ref, gb_ref, hsum_ref, code_ref, gsum_ref = refs[:7]
    refs = refs[7:]
    final_ref, blend_ref, rows_ref, gprev_ref, base_ref = refs[:5]
    gatt_refs = refs[5:9]
    nlow_ref, ilow_ref, gin_ref, gfeed_ref, gbranch_ref, vsum_ref, bsum_ref = refs[9:16]
    slope_ref, win_ref, wouter_ref, wout_ref, small_ref, sem = refs[16:22]
    buffers, row_sem = refs[22:26], refs[26]
    me = pl.program_id(0)

    def fetch(step):
        slot = lax.rem(step, 2)
        return [
            pltpu.make_async_copy(source.at[step], buffer.at[slot], row_sem.at[i, slot])
            for i, (source, buffer) in enumerate(zip((emb_ref, prev_ref, gt_ref, gb_ref), buffers))
        ]

    @pl.when(me == 0)
    def _():
        for one in fetch(0):
            one.start()

    @pl.when(me + 1 < pl.num_programs(0))
    def _():
        for one in fetch(me + 1):
            one.start()

    blocks, columns, width = win_ref.shape
    cut = wout_ref.shape[1] // 2
    core, zed, pair = info_ref[0], info_ref[1], info_ref[2]

    def load(firsts, seconds):
        copies = []

        def copy(source, start, size, target):
            copies.append(pltpu.make_async_copy(source.at[pl.ds(start, size)], target, sem.at[len(copies)]))

        for a in range(PAIRS):
            place = lax.rem(zed + a, PAIRS)
            order = jnp.bitwise_xor(place, pair)
            first, second = firsts[(-a) % PAIRS], seconds[a]
            copy(first, columns, cut, wout_ref.at[order, pl.ds(0, cut)])
            copy(second, width, cut, wout_ref.at[order, pl.ds(cut, cut)])
            copy(first, columns + cut, SMALL, small_ref.at[place])
            copy(first, 0, columns, win_ref.at[a])
            copy(second, 0, width, wouter_ref.at[a])
        for one in copies:
            one.start()
        for one in copies:
            one.wait()

    @pl.when((pl.program_id(0) == 0) & (core == 0))
    def _():
        load(mine, other)

    @pl.when((pl.program_id(0) == 0) & (core != 0))
    def _():
        load(other, mine)

    for one in fetch(me):
        one.wait()
    emb, prev, gt, gb = [buffer[lax.rem(me, 2)] for buffer in buffers]
    att = jnp.concatenate([ref[0] for ref in att_refs], axis=1)
    w_out = wout_ref[...].reshape(emb.shape[1], emb.shape[1])
    b_outer, g1, s1, g2, s2, halt = [
        jnp.concatenate([small_ref[a, i + 1 : i + 2, :WIDE] for a in range(PAIRS)], axis=1).astype(f32)
        for i in range(6)
    ]
    at = pl.ds(pl.program_id(0), 1)
    row = lax.broadcasted_iota(jnp.int32, (8, emb.shape[0]), 0)
    lines = jnp.where(row == 0, hsum_ref[at], jnp.where(row == 1, code_ref[at].astype(f32), gsum_ref[at]))
    cols = jnp.transpose(lines)
    sum_col, code_col, gsum_col = cols[:, 0:1], cols[:, 1:2], cols[:, 2:3]
    z1 = emb + dot(att, w_out)
    one, n1, i1 = norm_rows(z1, g1, s1)
    nlow = one.astype(bf16)
    nlow_ref[0] = nlow
    feed = None
    for j in range(blocks):
        pre = dot(nlow, win_ref[j]) + small_ref[lax.rem(zed + j, PAIRS), 0:1, :].astype(f32)
        act, slope = gelu_parts(pre)
        act = act.astype(bf16)
        ilow_ref[0, :, j * width : (j + 1) * width] = act
        slope_ref[:, j * width : (j + 1) * width] = slope
        part = dot(act, wouter_ref[j])
        feed = part if feed is None else feed + part
    z2 = one + (feed + b_outer)
    final, n2, i2 = norm_rows(z2, g2, s2)
    halt_logit = jnp.sum(emb * halt, axis=1, keepdims=True) + bhalt_ref[0, 0]
    halt_prob = jax.nn.sigmoid(halt_logit)
    running = (code_col > 0.5).astype(f32)
    halting = (code_col > 1.5).astype(f32)
    update = running * (halting * (1.0 - sum_col) + (1.0 - halting) * halt_prob)
    prev = prev.astype(f32)
    gb = gb.astype(f32)
    final_ref[0] = final.astype(bf16)
    blend_ref[0] = (prev * (1.0 - update) + final * update).astype(bf16)
    gprev_ref[0] = gb * (1.0 - update)
    g_update = jnp.sum(gb * (final - prev), axis=1, keepdims=True) + gsum_col
    g_halt_sum = gsum_col - running * halting * g_update
    g_logit = g_update * running * (1.0 - halting) * halt_prob * (1.0 - halt_prob)
    lane = lax.broadcasted_iota(jnp.int32, (emb.shape[0], WIDE), 1)
    packed = jnp.where(lane == 0, sum_col + update, jnp.where(lane == 1, g_halt_sum, 0.0))
    rows_ref[0] = jnp.transpose(packed)[0:8]
    gf = gt.astype(f32) + update * gb
    g_two = norm_back(gf, n2, i2, g2)
    gfeed = g_two.astype(bf16)
    gfeed_ref[0] = gfeed
    g_one = g_two
    for j in range(blocks):
        at = slice(j * width, (j + 1) * width)
        back = dot(gfeed, wouter_ref[j], NT)
        gin_f = back * slope_ref[:, at]
        gin = gin_f.astype(bf16)
        gin_ref[0, :, at] = gin
        bsum_ref[0, :, at] = jnp.sum(gin.astype(f32), axis=0, keepdims=True)
        g_one = g_one + dot(gin, win_ref[j], NT)
    g_emb = norm_back(g_one, n1, i1, g1)
    gbranch = g_emb.astype(bf16)
    gbranch_ref[0] = gbranch
    gatt = dot(gbranch, w_out, NT).astype(bf16)
    for d, ref in enumerate(gatt_refs):
        ref[0] = gatt[:, d * WIDE : (d + 1) * WIDE]
    base_ref[0] = g_emb + g_logit * halt
    total = lambda x: jnp.sum(x, axis=0, keepdims=True)
    logit_sum = jnp.broadcast_to(total(g_logit), (1, emb.shape[1]))
    vsum_ref[0] = jnp.concatenate(
        [
            total(gfeed.astype(f32)),
            total(g_one * n1),
            total(g_one),
            total(gf * n2),
            total(gf),
            total(g_logit * emb),
            logit_sum,
            jnp.zeros((1, emb.shape[1]), f32),
        ],
        axis=0,
    )


def dense(info, b_halt, mine, other, emb, att, prev, gt, gb, marks, part, out_rows):
    seqs, rows, width = emb.shape
    hidden = PAIRS * part
    outside = pl.BlockSpec(memory_space=pltpu.HBM)
    scalars = pl.BlockSpec(memory_space=pltpu.SMEM)
    rowspec = lambda w: pl.BlockSpec((1, rows, w), lambda s: (s, 0, 0))
    shape = lambda w, kind: jax.ShapeDtypeStruct((seqs, rows, w), kind)
    return pl.pallas_call(
        dense_kernel,
        grid=(seqs,),
        in_specs=[scalars, scalars]
        + [outside] * (2 * PAIRS)
        + [rowspec(WIDE)] * PAIRS
        + [outside] * 4
        + [full_spec(x) for x in marks],
        out_specs=[
            rowspec(width),
            rowspec(width),
            pl.BlockSpec((1, 8, rows), lambda s: (s, 0, 0)),
            rowspec(width),
            rowspec(width),
            rowspec(WIDE),
            rowspec(WIDE),
            rowspec(WIDE),
            rowspec(WIDE),
            rowspec(width),
            rowspec(hidden),
            rowspec(hidden),
            rowspec(width),
            rowspec(width),
            pl.BlockSpec((1, 8, width), lambda s: (s, 0, 0)),
            pl.BlockSpec((1, 1, hidden), lambda s: (s, 0, 0)),
        ],
        out_shape=[
            shape(width, bf16),
            shape(width, bf16),
            jax.ShapeDtypeStruct((seqs, 8, rows), f32),
            shape(width, f32),
            shape(width, f32),
            shape(WIDE, bf16),
            shape(WIDE, bf16),
            shape(WIDE, bf16),
            shape(WIDE, bf16),
            shape(width, bf16),
            shape(hidden, bf16),
            shape(hidden, bf16),
            shape(width, bf16),
            shape(width, bf16),
            jax.ShapeDtypeStruct((seqs, 8, width), f32),
            jax.ShapeDtypeStruct((seqs, 1, hidden), f32),
        ],
        scratch_shapes=[
            pltpu.VMEM((rows, hidden), f32),
            pltpu.VMEM((PAIRS, width, part), bf16),
            pltpu.VMEM((PAIRS, part, width), bf16),
            pltpu.VMEM((PAIRS, out_rows, width), bf16),
            pltpu.VMEM((PAIRS, SMALL, width), bf16),
            pltpu.SemaphoreType.DMA((5 * PAIRS,)),
            pltpu.VMEM((2, rows, width), f32),
            pltpu.VMEM((2, rows, width), bf16),
            pltpu.VMEM((2, rows, width), bf16),
            pltpu.VMEM((2, rows, width), bf16),
            pltpu.SemaphoreType.DMA((4, 2)),
        ],
        compiler_params=room(36),
        cost_estimate=cost(20),
        name="dense",
    )(info, b_halt, *mine, *other, *att, emb, prev, gt, gb, *marks)


def frequencies(half):
    return jnp.exp(-math.log(10000.0) * jnp.arange(half, dtype=f32) / (half - 1))


def position_rows(first, rows, columns):
    half = columns // 2
    freq = frequencies(half)[None, :]
    coarse = (first + 16 * jnp.arange(rows // 16, dtype=jnp.int32)).astype(f32)[:, None] * freq
    fine = jnp.arange(16, dtype=f32)[:, None] * freq
    sa, ca = jnp.sin(coarse)[:, None], jnp.cos(coarse)[:, None]
    sb, cb = jnp.sin(fine)[None], jnp.cos(fine)[None]
    both = jnp.concatenate([sa * cb + ca * sb, ca * cb - sa * sb], axis=2)
    return both.reshape(rows, columns)


def step_rows(columns):
    half = columns // 2
    angles = jnp.arange(4, dtype=f32)[:, None] * frequencies(half)[None, :]
    return jnp.concatenate([jnp.sin(angles), jnp.cos(angles)], axis=1)


def body(
    hidden_state,
    prev_state,
    halt_sum,
    halt_code,
    step_count,
    w_query,
    w_key,
    w_value,
    w_out,
    w_inner,
    b_inner,
    w_outer,
    b_outer,
    gain_attention,
    shift_attention,
    gain_feedforward,
    shift_feedforward,
    w_halt,
    b_halt,
    grad_transformed,
    grad_blended,
    grad_sum,
):
    seqs, rows, width = hidden_state.shape
    ctx = lax.axis_size("ctx")
    wsh = lax.axis_size("wsh")
    repeats = ctx // (2 * PAIRS)
    me = lax.axis_index("ctx")
    zed = lax.axis_index("wsh")
    core = me % 2
    pair = (me // 2) % PAIRS

    def swap(x, distance):
        return lax.ppermute(x, "ctx", [(i, i ^ distance) for i in range(ctx)])

    def sibling(x):
        return swap(x, 1)

    def partners(x, distance):
        return swap(x, 2 * distance)

    freq_rows = position_rows(me * rows, rows, width)
    table = step_rows(width)
    steps = step_count[:, :, None]
    step_signal = jnp.where(
        steps == 0, table[0], jnp.where(steps == 1, table[1], jnp.where(steps == 2, table[2], table[3]))
    )
    emb = hidden_state.astype(f32) + freq_rows[None] + step_signal
    emb_low = emb.astype(bf16)

    after = lambda x, *others: lax.optimization_barrier((x,) + others)[0]

    info = jnp.stack([core, zed, pair]).astype(jnp.int32)
    ring = [
        (c * wsh + z, c * wsh + (z + (1 if c % 2 == 0 else -1)) % wsh) for c in range(ctx) for z in range(wsh)
    ]
    turn = lambda x: lax.ppermute(x, ("ctx", "wsh"), ring)
    out_rows = w_out.shape[0]
    part = w_inner.shape[1]
    half = rows // 2

    tokens = [emb_low] + [partners(emb_low, d) for d in (1, 2)]
    pair_of = lambda c: (c // 2) % PAIRS
    held = pack(info, [w_query, w_key, w_value])
    hop = lambda x, starts, step: lax.ppermute(
        x,
        ("ctx", "wsh"),
        [(c * wsh + (pair_of(c) ^ z), c * wsh + (pair_of(c) ^ z ^ step)) for c in range(ctx) for z in starts],
    )
    near = jnp.where(zed == pair, held, hop(held, (0,), 1))
    far = hop(near, (0, 1), 2)
    tokens.append(partners(tokens[2][:, :half], 1))
    tokens.append(partners(tokens[1][:, half:], 2))
    vectors = [b_outer, gain_attention, shift_attention, gain_feedforward, shift_feedforward, w_halt]
    feed = pack_feed(after(info, held), w_inner, w_outer, w_out, b_inner, vectors)
    feed_mine = [feed, turn(feed)]
    chosen = choose(after(info, feed_mine[1], *tokens[1:3]), near, far)
    w_mine = assemble(info, chosen, sibling(chosen))

    groups = [[r * 2 * PAIRS + i for r in range(repeats)] for i in range(2 * PAIRS)]
    q_list, kvs_list, fold = [], [], None
    w_now = w_mine
    own_list = []
    for s in range(seqs):
        q, own = project(s, tokens, w_now)
        w_now = after(w_mine, q)
        q_list.append(q)
        own_list.append(own)

    def keys_values(own):
        other = sibling(own)
        if repeats == 1:
            return [own, other]
        both = jnp.concatenate([own, other], axis=1)
        return [lax.all_gather(both, "ctx", axis=1, tiled=True, axis_index_groups=groups)]

    feed_mine.append(turn(feed_mine[1]))
    kvs_list = [keys_values(own) for own in own_list]
    fold = attend(0, seqs, q_list[0], kvs_list[0], None)
    feed_mine.append(turn(after(feed_mine[2], fold[1])))
    fold = attend(1, seqs, after(q_list[1], feed_mine[2], kvs_list[2][-1]), kvs_list[1], fold)
    feed_other = [sibling(after(x, fold[1])) for x in feed_mine[:2]]
    fold = attend(2, seqs, after(q_list[2], *feed_other), kvs_list[2], fold)
    o32, mass, *low = fold
    att = [low[0]] + [partners(low[d], d) for d in range(1, PAIRS)]
    feed_other.append(sibling(after(feed_mine[2], mass)))
    feed_other.append(sibling(after(feed_mine[3], *att[1:])))
    w_order = [w_mine] + [partners(after(w_mine, *att[1:]), d) for d in range(1, PAIRS)]

    (
        final,
        blended,
        row_out,
        grad_prev,
        base,
        gatt0,
        gatt1,
        gatt2,
        gatt3,
        nlow,
        ilow,
        gin,
        gfeed,
        gbranch,
        vsum,
        bsum,
    ) = dense(
        info, b_halt.reshape(1, 1), feed_mine, feed_other, emb, att, prev_state, grad_transformed, grad_blended,
        [halt_sum, halt_code, grad_sum], part, out_rows,
    )
    new_sum = row_out[:, 0]
    grad_halt_sum = row_out[:, 1]
    gs = [gatt0] + [partners(x, d + 1) for d, x in enumerate((gatt1, gatt2, gatt3))]

    keep_a, give_a = outer_grads(after(info, vsum, *w_order[1:]), att, ilow, gfeed, gbranch, ctx)
    keep_b, give_b = inner_grads(after(info, keep_a), nlow, gin, vsum, bsum, ctx)
    joined_a = join(after(keep_a, keep_b), sibling(give_a), False)

    def spread_pieces(pieces):
        return [pieces[0]] + [partners(pieces[d], d) for d in range(1, PAIRS)]

    shared_a = spread_pieces(joined_a)

    kinds = [f32, bf16] if repeats == 1 else [bf16]

    def split_back(s, token):
        dq, *dkv = attend_back(s, q_list[s], gs, o32, token, kvs_list[s], kinds)
        if repeats == 1:
            kept, sent = dkv
        else:
            summed = lax.psum_scatter(
                dkv[0], "ctx", scatter_dimension=1, tiled=True, axis_index_groups=groups
            )
            kept, sent = summed[:, : PAIRS * rows].astype(f32), summed[:, PAIRS * rows :]
        return dq, kept, sent

    backs = [split_back(0, after(mass, *joined_a))]
    joined_b = join(after(keep_b, backs[0][0], *shared_a), sibling(give_b), True)
    shared_b = spread_pieces(joined_b)
    backs.append(split_back(1, after(mass, *joined_b)))
    got = lambda back, *others: back[:2] + (sibling(after(back[2], *others)),)
    share_keep, share_send = share_parts(after(info, backs[1][0]), shared_a, shared_b)
    if repeats > 1:
        share_keep, share_send = (
            lax.psum_scatter(x, "ctx", scatter_dimension=0, tiled=True, axis_index_groups=groups)
            for x in (share_keep, share_send)
        )
    cross = lambda x, step: lax.ppermute(x, "wsh", [(z, z ^ step) for z in range(wsh)])
    moved = cross(share_send[0], 1)
    *pieces, gq = combine(
        after(info, share_keep), (0, 1), tokens, [got(backs[0]), got(backs[1], share_keep)], None, False
    )
    blocks = spread_pieces(pieces)
    backs.append(split_back(2, after(mass, gq)))
    own, sent = halve(after(share_keep[0], backs[2][0], *blocks[1:]), moved)
    made = combine(info, (2,), tokens, [got(backs[2], own)], gq, repeats == 1)
    pieces, keep, give = made[:PAIRS], made[PAIRS], made[-1]
    block = [pieces[0]] + [partners(pieces[d], d) for d in (1, 2)]
    if repeats == 1:
        heads = share_small(after(info, *block), sent, spread_pieces(join_small(keep, sibling(give))))
        block.append(partners(after(pieces[3], heads[0]), 3))
        heads = [heads[0]] + [cross(heads[step], step) for step in range(1, wsh)]
        grad_state = add_state(0, after(base, heads[0]), blocks, w_order)
        share = total_parts(after(own, grad_state), heads)
        grad_state = add_state(2, after(grad_state, share), block, w_order)
        mine = spread_pieces([share] * PAIRS)
        (grad_w_outer, grad_w_out, grad_w_inner, tail, grad_w_query, grad_w_key, grad_w_value) = unpack(
            info, mine, [sibling(after(x, grad_state)) for x in mine], part, out_rows
        )
    else:
        block.append(partners(pieces[3], 3))
        share = total_parts(own, [cross(sent, 2)])
        grad_state = add_state(2, add_state(0, base, blocks, w_order), block, w_order)
        whole = lax.all_gather(share, "ctx", axis=0).astype(f32)
        a, b, c = part // ctx, out_rows // ctx, width // ctx
        grad_w_outer = whole[:, :a].reshape(part, width)
        grad_w_out = whole[:, a : a + b].reshape(out_rows, width)
        grad_w_inner = whole[:, a + b : a + b + c].reshape(width, part)
        tail = whole[0, a + b + c :]
        own = lax.dynamic_update_index_in_dim(jnp.zeros((wsh,) + keep.shape, f32), keep, pair, 0)
        own = lax.psum(lax.psum_scatter(own.astype(bf16), "wsh", scatter_dimension=0).astype(f32), "ctx")
        grad_w_query, grad_w_key, grad_w_value = (own[:, i * WIDE : (i + 1) * WIDE] for i in range(3))
    grad_b_inner = tail[7]
    vec_grads = [tail[i, :out_rows] for i in range(6)]
    grad_b_halt = tail[6, :1] + tail[6, WIDE : WIDE + 1]

    return (
        final,
        blended,
        new_sum,
        grad_state,
        grad_prev,
        grad_halt_sum,
        grad_w_query,
        grad_w_key,
        grad_w_value,
        grad_w_out,
        grad_w_inner,
        grad_b_inner,
        grad_w_outer,
        vec_grads[0],
        vec_grads[1],
        vec_grads[2],
        vec_grads[3],
        vec_grads[4],
        vec_grads[5],
        grad_b_halt,
    )


def solution(mesh):
    rows = P("wsh", "ctx", None)
    marks = P("wsh", "ctx")
    column, row, vector = P(None, "wsh"), P("wsh", None), P("wsh")
    in_specs = (
        (rows, rows, marks, marks, marks, column, column, column, row, column, vector, row)
        + (vector,) * 6
        + (P(), rows, rows, marks)
    )
    out_specs = (
        (rows, rows, marks, rows, rows, marks, column, column, column, row, column, vector, row)
        + (vector,) * 6
        + (P(),)
    )
    return jax.shard_map(body, mesh=mesh, in_specs=in_specs, out_specs=out_specs, check_vma=False)
```

profile of v0, /device:TPU:0, one launch (start us, length us, event | category | flops | bytes accessed | tf_op | source)
XLA Modules:
  0.0 226.5 jit_solution(17333904478314177465)
XLA Ops:
  2.5 3.0 %collective-permute-start.2 = (bf16[3,256,512]{2,1,0:T(8,128)(2,1)S(1)}, bf16[3,256,512]{2,1,0:T(8,128)(2,1)S(1)}, u32[]{:S(2)}, u32[]{:S(2)}) collective-permute-start(bf16[3,256,512]{2,1,0:T(8,128)(2,1)S(1)} %get-tuple-element.269.refs_0_), channel_id=1, source_target_pairs={{0,8},{4,12},{8,0},{12,4},{16,24},{20,28},{24,16},{28,20},{1,9},{5... | collective-permute-start | bytes 2359304 | tf_op jit(solution)/shard_map/ppermute | solution.py:1088
  5.5 1.5 collective-permute-start.3
  9.6 3.5 %collective-permute-start.6 = (bf16[256,384]{1,0:T(8,128)(2,1)S(1)}, bf16[256,384]{1,0:T(8,128)(2,1)S(1)}, u32[]{:S(2)}, u32[]{:S(2)}) collective-permute-start(bf16[256,384]{1,0:T(8,128)(2,1)S(1)} %pack.1), channel_id=1, source_target_pairs={{0,1},{4,5},{9,8},{13,12},{18,19},{22,23},{27,26},{31,30}} | collective-permute-start | bytes 589832 | tf_op jit(solution)/shard_map/ppermute | solution.py:1119
  14.6 3.7 %collective-permute-done.6 = bf16[256,384]{1,0:T(8,128)(2,1)S(1)} collective-permute-done((bf16[256,384]{1,0:T(8,128)(2,1)S(1)}, bf16[256,384]{1,0:T(8,128)(2,1)S(1)}, u32[]{:S(2)}, u32[]{:S(2)}) %collective-permute-start.6) | collective-permute-done | bytes 196640 | tf_op jit(solution)/shard_map/ppermute | solution.py:1119
  19.7 4.9 %collective-permute-done.3.refs_2_ = bf16[3,256,512]{2,1,0:T(8,128)(2,1)} collective-permute-done((bf16[3,256,512]{2,1,0:T(8,128)(2,1)S(1)}, bf16[3,256,512]{2,1,0:T(8,128)(2,1)}, u32[]{:S(2)}, u32[]{:S(2)}) %collective-permute-start.3) | collective-permute-done | bytes 786464 | tf_op jit(solution)/shard_map/ppermute | solution.py:1088
  26.1 1.8 collective-permute-start.5
  27.9 3.6 %collective-permute-done.refs_1_ = bf16[592,512]{1,0:T(8,128)(2,1)} collective-permute-done((bf16[592,512]{1,0:T(8,128)(2,1)}, bf16[592,512]{1,0:T(8,128)(2,1)}, u32[]{:S(2)}, u32[]{:S(2)}) %collective-permute-start) | collective-permute-done | bytes 606240 | tf_op jit(solution)/shard_map/ppermute | solution.py:1111
  31.5 2.4 %collective-permute-done.7.far_ref = bf16[256,384]{1,0:T(8,128)(2,1)S(1)} collective-permute-done((bf16[256,384]{1,0:T(8,128)(2,1)S(1)}, bf16[256,384]{1,0:T(8,128)(2,1)S(1)}, u32[]{:S(2)}, u32[]{:S(2)}) %collective-permute-start.7) | collective-permute-done | bytes 196640 | tf_op jit(solution)/shard_map/ppermute | solution.py:1119
  34.5 3.9 %collective-permute-start.1 = (bf16[592,512]{1,0:T(8,128)(2,1)}, bf16[592,512]{1,0:T(8,128)(2,1)S(1)}, u32[]{:S(2)}, u32[]{:S(2)}) collective-permute-start(bf16[592,512]{1,0:T(8,128)(2,1)} %collective-permute-done.refs_1_), channel_id=1, source_target_pairs={{0,1},{1,2},{2,3},{3,0},{4,7},{5,4},{6,5},{7,6},{8,9},{9,10},{10,1... | collective-permute-start | bytes 1818632 | tf_op jit(solution)/shard_map/ppermute | solution.py:1111
  39.0 1.7 project.3
  40.7 3.0 %collective-permute-start.9 = (bf16[1,1024,256]{2,1,0:T(8,128)(2,1)S(1)}, bf16[1,1024,256]{2,1,0:T(8,128)(2,1)S(1)}, u32[]{:S(2)}, u32[]{:S(2)}) collective-permute-start(bf16[1,1024,256]{2,1,0:T(8,128)(2,1)S(1)} %get-tuple-element.147.refs_0_.refs_6_), channel_id=1, source_target_pairs={{0,4},{4,0},{8,12},{12,8},{16,20},{20,16},{24,28},{28,24},{1,5},{5... | collective-permute-start | bytes 1572872 | tf_op jit(solution)/shard_map/ppermute | solution.py:1088
  43.7 1.7 project.4
  45.4 1.7 project.5
  47.6 6.6 %attend.3 = (f32[3,1024,128]{2,1,0:T(8,128)S(1)}, f32[3,8,1024]{2,1,0:T(8,128)S(1)}, bf16[3,256,128]{2,1,0:T(8,128)(2,1)S(1)}, bf16[3,256,128]{2,1,0:T(8,128)(2,...) custom-call(bf16[1,1024,128]{2,1,0:T(8,128)(2,1)S(1)} %get-tuple-element.146.q_ref, ...), custom_call_target="tpu_custom_call" | custom-call | flops 1100000000 | bytes 1024 | tf_op jit(solution)/shard_map/attend/pallas_call | solution.py:155
  54.2 1.5 collective-permute-done.1.refs_2_
  55.7 6.0 %attend.4 = (f32[3,1024,128]{2,1,0:T(8,128)S(1)}, f32[3,8,1024]{2,1,0:T(8,128)S(1)}, bf16[3,256,128]{2,1,0:T(8,128)(2,1)S(1)}, bf16[3,256,128]{2,1,0:T(8,128)(2,...) custom-call(bf16[1,1024,128]{2,1,0:T(8,128)(2,1)S(1)} %get-tuple-ele, ...), custom_call_target="tpu_custom_call", output_to_operand_aliasing={{0}: (3, {}), {1}: (4, {}), {2}: (5, {}), {3}: (6, {}), {4}... | custom-call | flops 1100000000 | bytes 1024 | tf_op jit(solution)/shard_map/attend/pallas_call | solution.py:155
  62.3 1.7 collective-permute-done.13.refs_4_
  65.0 6.3 %attend.5 = (f32[3,1024,128]{2,1,0:T(8,128)S(1)}, f32[3,8,1024]{2,1,0:T(8,128)S(1)}, bf16[3,256,128]{2,1,0:T(8,128)(2,1)S(1)}, bf16[3,256,128]{2,1,0:T(8,128)(2,...) custom-call(bf16[1,1024,128]{2,1,0:T(8,128)(2,1)S(1)} %get-tuple-ele, ...), custom_call_target="tpu_custom_call", output_to_operand_aliasing={{0}: (3, {}), {1}: (4, {}), {2}: (5, {}), {3}: (6, {}), {4}... | custom-call | flops 1100000000 | bytes 1024 | tf_op jit(solution)/shard_map/attend/pallas_call | solution.py:155
  72.0 2.8 %collective-permute-start.18 = (bf16[3,256,128]{2,1,0:T(8,128)(2,1)S(1)}, bf16[3,256,128]{2,1,0:T(8,128)(2,1)S(1)}, u32[]{:S(2)}, u32[]{:S(2)}) collective-permute-start(bf16[3,256,128]{2,1,0:T(8,128)(2,1)S(1)} %get-tuple-element.175), channel_id=1, source_target_pairs={{0,24},{4,28},{8,16},{12,20},{16,8},{20,12},{24,0},{28,4},{1,25},{... | collective-permute-start | bytes 589832 | tf_op jit(solution)/shard_map/ppermute | solution.py:1088
  74.8 3.7 %collective-permute-done.10.refs_3_ = bf16[592,512]{1,0:T(8,128)(2,1)S(1)} collective-permute-done((bf16[592,512]{1,0:T(8,128)(2,1)S(1)}, bf16[592,512]{1,0:T(8,128)(2,1)S(1)}, u32[]{:S(2)}, u32[]{:S(2)}) %collective-permute-start.10) | collective-permute-done | bytes 606240 | tf_op jit(solution)/shard_map/ppermute | solution.py:1111
  79.1 3.8 %collective-permute-done.17.refs_10_.a2_ref = bf16[3,256,128]{2,1,0:T(8,128)(2,1)S(1)} collective-permute-done((bf16[3,256,128]{2,1,0:T(8,128)(2,1)S(1)}, bf16[3,256,128]{2,1,0:T(8,128)(2,1)S(1)}, u32[]{:S(2)}, u32[]{:S(2)}) %collective-permute-start.17) | collective-permute-done | bytes 196640 | tf_op jit(solution)/shard_map/ppermute | solution.py:1088
  85.3 1.8 collective-permute-start.25
  87.1 18.5 %dense.1 = (bf16[3,256,512]{2,1,0:T(8,128)(2,1)}, bf16[3,256,512]{2,1,0:T(8,128)(2,1)}, f32[3,8,256]{2,1,0:T(8,128)S(1)}, f32[3,256,512]{2,1,0:T(8,128)}, f32[3,...) custom-call(s32[3]{0:T(128)S(1)} %pad_add_fusion.info_ref, ...), custom_call_target="tpu_custom_call" | custom-call | flops 22000001024 | bytes 1024 | tf_op jit(solution)/shard_map/dense/pallas_call | solution.py:970
  105.6 4.2 %outer_grads.1 = (bf16[4,1,4,80,512]{4,3,2,1,0:T(8,128)(2,1)S(1)}, bf16[4,1,4,80,512]{4,3,2,1,0:T(8,128)(2,1)S(1)}) custom-call(s32[3]{0:T(128)S(1)} %pad_add_fusion.info_ref, bf16[3,256,128]{2,1,0:T(8,128)(2,1)S(1)} %get-tuple-element.177.refs_8_.a0_ref, bf16[3,256,128]{2,1,0:T(8,128)(2,1)S(1)} %collective-permute-done.16.refs_9_.a1_ref, ...), custom_call_target="tpu_custom_call" | custom-call | flops 4950000128 | bytes 1024 | tf_op jit(solution)/shard_map/outer_grads/pallas_call | solution.py:611
  111.8 1.8 collective-permute-start.22
  113.5 4.0 %inner_grads.1 = (bf16[4,1,4,72,512]{4,3,2,1,0:T(8,128)(2,1)S(1)}, bf16[4,1,4,72,512]{4,3,2,1,0:T(8,128)(2,1)S(1)}) custom-call(s32[3]{0:T(128)S(1)} %pad_add_fusion.info_ref, bf16[3,256,512]{2,1,0:T(8,128)(2,1)S(1)} %get-tuple-element.195.nlow_ref, bf16[3,256,2048]{2,1,0:T(8,128)(2,1)S(1)} %copy-done.18, f32[3,8,512]{2,1,0:T(8,128)S(1)} %get-tuple-element.187.vsum_ref, ...), custom_call_target="tpu_custom_call" | custom-call | flops 4950000128 | bytes 1024 | tf_op jit(solution)/shard_map/inner_grads/pallas_call | solution.py:611
  118.2 1.4 collective-permute-start.27
  120.0 2.6 %collective-permute-done.21.refs_2_ = bf16[3,256,128]{2,1,0:T(8,128)(2,1)S(1)} collective-permute-done((bf16[3,256,128]{2,1,0:T(8,128)(2,1)S(1)}, bf16[3,256,128]{2,1,0:T(8,128)(2,1)S(1)}, u32[]{:S(2)}, u32[]{:S(2)}) %collective-permute-start.21) | collective-permute-done | bytes 196640 | tf_op jit(solution)/shard_map/ppermute | solution.py:1088
  122.7 12.5 %attend_back.3 = (bf16[1,1024,128]{2,1,0:T(8,128)(2,1)S(1)}, f32[1,1024,256]{2,1,0:T(8,128)S(1)}, bf16[1,1024,256]{2,1,0:T(8,128)(2,1)S(1)}) custom-call(bf16[1,1024,128]{2,1,0:T(8,128)(2,1)S(1)} %get-tuple-element.146.q_ref, bf16[3,256,128]{2,1,0:T(8,128)(2,1)S(1)} %get-tuple-element.182.refs_0_, bf16[3,256,128]{2,1,0:T(8,128)(2,1)S(1)} %collective-permute-done.20.refs_1_, ...), custom_call_target="tpu_custom_call" | custom-call | flops 15399999488 | bytes 1024 | tf_op jit(solution)/shard_map/attend_back/pallas_call | solution.py:237
  137.9 1.5 collective-permute-start.32
  140.8 12.9 %attend_back.4 = (bf16[1,1024,128]{2,1,0:T(8,128)(2,1)S(1)}, f32[1,1024,256]{2,1,0:T(8,128)S(1)}, bf16[1,1024,256]{2,1,0:T(8,128)(2,1)S(1)}) custom-call(bf16[1,1024,128]{2,1,0:T(8,128)(2,1)S(1)} %get-tuple-element.154.q_ref, bf16[3,256,128]{2,1,0:T(8,128)(2,1)S(1)} %get-tuple-element.182.refs_0_, bf16[3,256,128]{2,1,0:T(8,128)(2,1)S(1)} %collective-permute-done.20.refs_1_, ...), custom_call_target="tpu_custom_call" | custom-call | flops 15399999488 | bytes 1024 | tf_op jit(solution)/shard_map/attend_back/pallas_call | solution.py:237
  154.7 1.8 collective-permute-done.35.refs_10_
  156.5 2.6 %combine.2 = (bf16[2,256,384]{2,1,0:T(8,128)(2,1)S(1)}, bf16[2,256,384]{2,1,0:T(8,128)(2,1)S(1)}, bf16[2,256,384]{2,1,0:T(8,128)(2,1)S(1)}, bf16[2,256,384]{2,1,0:T(8,128)(2,1)S(1)}, f32[512,384]{1,0:T(8,128)S(1)}) custom-call(s32[3]{0:T(128)S(1)} %pad_add_fusion.info_ref, bf16[3,256,512]{2,1,0:T(8,128)(2,1)S(1)} %get-tuple-element.269.refs_0_, ...), custom_call_target="tpu_custom_call" | custom-call | flops 2200000000 | bytes 1024 | tf_op jit(solution)/shard_map/combine/pallas_call | solution.py:410
  162.7 12.7 %attend_back.5 = (bf16[1,1024,128]{2,1,0:T(8,128)(2,1)S(1)}, f32[1,1024,256]{2,1,0:T(8,128)S(1)}, bf16[1,1024,256]{2,1,0:T(8,128)(2,1)S(1)}) custom-call(bf16[1,1024,128]{2,1,0:T(8,128)(2,1)S(1)} %get-tuple-element.165.q_ref, bf16[3,256,128]{2,1,0:T(8,128)(2,1)S(1)} %get-tuple-element.182.refs_0_, bf16[3,256,128]{2,1,0:T(8,128)(2,1)S(1)} %collective-permute-done.20.refs_1_, ...), custom_call_target="tpu_custom_call" | custom-call | flops 15399999488 | bytes 1024 | tf_op jit(solution)/shard_map/attend_back/pallas_call | solution.py:237
  175.4 2.8 %collective-permute-done.37.refs_2_ = bf16[2,256,384]{2,1,0:T(8,128)(2,1)S(1)} collective-permute-done((bf16[2,256,384]{2,1,0:T(8,128)(2,1)S(1)}, bf16[2,256,384]{2,1,0:T(8,128)(2,1)S(1)}, u32[]{:S(2)}, u32[]{:S(2)}) %collective-permute-start.37) | collective-permute-done | bytes 393248 | tf_op jit(solution)/shard_map/ppermute | solution.py:1088
  179.6 1.9 collective-permute-done.40.refs_7_
  181.5 2.1 combine.3
  187.9 1.7 collective-permute-start.46
  189.7 1.8 collective-permute-done.41.refs_1_
  194.8 2.6 %collective-permute-start.48 = (bf16[200,512]{1,0:T(8,128)(2,1)S(1)}, bf16[200,512]{1,0:T(8,128)(2,1)S(1)}, u32[]{:S(2)}, u32[]{:S(2)}) collective-permute-start(bf16[200,512]{1,0:T(8,128)(2,1)S(1)} %get-tuple-element.251), channel_id=1, source_target_pairs={{0,2},{1,3},{2,0},{3,1},{4,6},{5,7},{6,4},{7,5},{8,10},{9,11},{10,... | collective-permute-start | bytes 614408 | tf_op jit(solution)/shard_map/ppermute | solution.py:1222
  197.4 1.6 collective-permute-start.49
  199.0 1.6 collective-permute-start.50
  200.5 3.3 %add_state.2.base_ref = f32[3,256,512]{2,1,0:T(8,128)} custom-call(f32[3,256,512]{2,1,0:T(8,128)} %get-tuple-element.247.base_ref, bf16[2,256,384]{2,1,0:T(8,128)(2,1)S(1)} %get-tuple-element.248.refs_0_, bf16[2,256,384]{2,1,0:T(8,128)(2,1)S(1)} %collective-permute-done.36.refs_1_, ...), custom_call_target="tpu_custom_call", output_to_operand_aliasing={{}: (0, {})} | custom-call | flops 5500000256 | bytes 1024 | tf_op jit(solution)/shard_map/add_state/pallas_call | solution.py:490
  204.3 3.3 %collective-permute-done.48.refs_2_ = bf16[200,512]{1,0:T(8,128)(2,1)S(1)} collective-permute-done((bf16[200,512]{1,0:T(8,128)(2,1)S(1)}, bf16[200,512]{1,0:T(8,128)(2,1)S(1)}, u32[]{:S(2)}, u32[]{:S(2)}) %collective-permute-start.48) | collective-permute-done | bytes 204832 | tf_op jit(solution)/shard_map/ppermute | solution.py:1222
  209.6 1.6 collective-permute-start.53
  211.2 2.6 %add_state.3 = f32[3,256,512]{2,1,0:T(8,128)} custom-call(f32[3,256,512]{2,1,0:T(8,128)} %add_state.2.base_ref, bf16[1,256,384]{2,1,0:T(8,128)(2,1)S(1)} %get-tuple-element.235.refs_0_, bf16[1,256,384]{2,1,0:T(8,128)(2,1)S(1)} %collective-permute-done.41.refs_1_, ...), custom_call_target="tpu_custom_call", output_to_operand_aliasing={{}: (0, {})} | custom-call | flops 2750000128 | bytes 1024 | tf_op jit(solution)/shard_map/add_state/pallas_call | solution.py:490
  215.0 3.0 %collective-permute-done.52.refs_2_ = bf16[200,512]{1,0:T(8,128)(2,1)S(1)} collective-permute-done((bf16[200,512]{1,0:T(8,128)(2,1)S(1)}, bf16[200,512]{1,0:T(8,128)(2,1)S(1)}, u32[]{:S(2)}, u32[]{:S(2)}) %collective-permute-start.52) | collective-permute-done | bytes 204832 | tf_op jit(solution)/shard_map/ppermute | solution.py:1088
  219.7 2.4 %unpack.1 = (f32[512,512]{1,0:T(8,128)}, f32[128,512]{1,0:T(8,128)}, f32[512,512]{1,0:T(8,128)}, f32[8,512]{1,0:T(8,128)S(1)}, f32[512,128]{1,0:T(8,128)}, /*index=5*/f32[512,128]{1,0:T(8,128)}, f32[512,128]{1,0:T(8,128)}) custom-call(s32[3]{0:T(128)S(1)} %pad_add_fusion.info_ref, bf16[200,512]{1,0:T(8,128)(2,1)S(1)} %total.1.refs_0_, ...), custom_call_target="tpu_custom_call" | custom-call | flops 3300000000 | bytes 1024 | tf_op jit(solution)/shard_map/unpack/pallas_call | solution.py:786
  (157 shorter events, 42.8 us)
Async XLA Ops:
  2.5 23.6 %collective-permute-start.2 = (bf16[3,256,512]{2,1,0:T(8,128)(2,1)S(1)}, bf16[3,256,512]{2,1,0:T(8,128)(2,1)S(1)}, u32[]{:S(2)}, u32[]{:S(2)}) collective-permute-start(bf16[3,256,512]{2,1,0:T(8,128)(2,1)S(1)} %get-tuple-element.269.refs_0_), channel_id=1, source_target_pairs={{0,8},{4,12},{8,0},{12,4},{16,24},{20,28},{24,16},{28,20},{1,9},{5... | collective-permute-start | bytes 2359304 | tf_op jit(solution)/shard_map/ppermute | solution.py:1088
  5.5 19.1 %collective-permute-start.3 = (bf16[3,256,512]{2,1,0:T(8,128)(2,1)S(1)}, bf16[3,256,512]{2,1,0:T(8,128)(2,1)}, u32[]{:S(2)}, u32[]{:S(2)}) collective-permute-start(bf16[3,256,512]{2,1,0:T(8,128)(2,1)S(1)} %get-tuple-element.269.refs_0_), channel_id=1, source_target_pairs={{0,16},{4,20},{8,24},{12,28},{16,0},{20,4},{24,8},{28,12},{1,17},{... | collective-permute-start | bytes 2359304 | tf_op jit(solution)/shard_map/ppermute | solution.py:1088
  9.6 8.7 %collective-permute-start.6 = (bf16[256,384]{1,0:T(8,128)(2,1)S(1)}, bf16[256,384]{1,0:T(8,128)(2,1)S(1)}, u32[]{:S(2)}, u32[]{:S(2)}) collective-permute-start(bf16[256,384]{1,0:T(8,128)(2,1)S(1)} %pack.1), channel_id=1, source_target_pairs={{0,1},{4,5},{9,8},{13,12},{18,19},{22,23},{27,26},{31,30}} | collective-permute-start | bytes 589832 | tf_op jit(solution)/shard_map/ppermute | solution.py:1119
  14.6 16.8 %collective-permute-start = (bf16[592,512]{1,0:T(8,128)(2,1)}, bf16[592,512]{1,0:T(8,128)(2,1)}, u32[]{:S(2)}, u32[]{:S(2)}) collective-permute-start(bf16[592,512]{1,0:T(8,128)(2,1)} %pack_feed.1.refs_0_), channel_id=1, source_target_pairs={{0,1},{1,2},{2,3},{3,0},{4,7},{5,4},{6,5},{7,6},{8,9},{9,10},{10,1... | collective-permute-start | bytes 1818632 | tf_op jit(solution)/shard_map/ppermute | solution.py:1111
  18.4 15.5 %collective-permute-start.7 = (bf16[256,384]{1,0:T(8,128)(2,1)S(1)}, bf16[256,384]{1,0:T(8,128)(2,1)S(1)}, u32[]{:S(2)}, u32[]{:S(2)}) collective-permute-start(bf16[256,384]{1,0:T(8,128)(2,1)S(1)} %broadcast_select_fusion.near_ref), channel_id=1, source_target_pairs={{0,2},{1,3},{4,6},{5,7},{9,11},{8,10},{13,15},{12,14},{18,16},{19,... | collective-permute-start | bytes 589832 | tf_op jit(solution)/shard_map/ppermute | solution.py:1119
  25.7 13.3 %collective-permute-start.4 = (bf16[3,128,512]{2,1,0:T(8,128)(2,1)S(1)}, bf16[3,128,512]{2,1,0:T(8,128)(2,1)S(1)}, u32[]{:S(2)}, u32[]{:S(2)}) collective-permute-start(bf16[3,128,512]{2,1,0:T(8,128)(2,1)S(1)} %slice.74), channel_id=1, source_target_pairs={{0,8},{4,12},{8,0},{12,4},{16,24},{20,28},{24,16},{28,20},{1,9},{5... | collective-permute-start | bytes 1179656 | tf_op jit(solution)/shard_map/ppermute | solution.py:1088
  26.1 12.9 %collective-permute-start.5 = (bf16[3,128,512]{2,1,0:T(8,128)(2,1)S(1)}, bf16[3,128,512]{2,1,0:T(8,128)(2,1)S(1)}, u32[]{:S(2)}, u32[]{:S(2)}) collective-permute-start(bf16[3,128,512]{2,1,0:T(8,128)(2,1)S(1)} %slice.75), channel_id=1, source_target_pairs={{0,16},{4,20},{8,24},{12,28},{16,0},{20,4},{24,8},{28,12},{1,17},{... | collective-permute-start | bytes 1179656 | tf_op jit(solution)/shard_map/ppermute | solution.py:1088
  34.5 21.2 %collective-permute-start.1 = (bf16[592,512]{1,0:T(8,128)(2,1)}, bf16[592,512]{1,0:T(8,128)(2,1)S(1)}, u32[]{:S(2)}, u32[]{:S(2)}) collective-permute-start(bf16[592,512]{1,0:T(8,128)(2,1)} %collective-permute-done.refs_1_), channel_id=1, source_target_pairs={{0,1},{1,2},{2,3},{3,0},{4,7},{5,4},{6,5},{7,6},{8,9},{9,10},{10,1... | collective-permute-start | bytes 1818632 | tf_op jit(solution)/shard_map/ppermute | solution.py:1111
  40.7 7.0 %collective-permute-start.9 = (bf16[1,1024,256]{2,1,0:T(8,128)(2,1)S(1)}, bf16[1,1024,256]{2,1,0:T(8,128)(2,1)S(1)}, u32[]{:S(2)}, u32[]{:S(2)}) collective-permute-start(bf16[1,1024,256]{2,1,0:T(8,128)(2,1)S(1)} %get-tuple-element.147.refs_0_.refs_6_), channel_id=1, source_target_pairs={{0,4},{4,0},{8,12},{12,8},{16,20},{20,16},{24,28},{28,24},{1,5},{5... | collective-permute-start | bytes 1572872 | tf_op jit(solution)/shard_map/ppermute | solution.py:1088
  47.1 8.6 %collective-permute-start.11 = (bf16[1,1024,256]{2,1,0:T(8,128)(2,1)S(1)}, bf16[1,1024,256]{2,1,0:T(8,128)(2,1)S(1)}, u32[]{:S(2)}, u32[]{:S(2)}) collective-permute-start(bf16[1,1024,256]{2,1,0:T(8,128)(2,1)S(1)} %get-tuple-element.153.refs_0_.refs_6_), channel_id=1, source_target_pairs={{0,4},{4,0},{8,12},{12,8},{16,20},{20,16},{24,28},{28,24},{1,5},{5... | collective-permute-start | bytes 1572872 | tf_op jit(solution)/shard_map/ppermute | solution.py:1088
  47.2 8.6 %collective-permute-start.12 = (bf16[1,1024,256]{2,1,0:T(8,128)(2,1)S(1)}, bf16[1,1024,256]{2,1,0:T(8,128)(2,1)S(1)}, u32[]{:S(2)}, u32[]{:S(2)}) collective-permute-start(bf16[1,1024,256]{2,1,0:T(8,128)(2,1)S(1)} %get-tuple-element.155.refs_0_.refs_6_), channel_id=1, source_target_pairs={{0,4},{4,0},{8,12},{12,8},{16,20},{20,16},{24,28},{28,24},{1,5},{5... | collective-permute-start | bytes 1572872 | tf_op jit(solution)/shard_map/ppermute | solution.py:1088
  62.3 16.2 %collective-permute-start.10 = (bf16[592,512]{1,0:T(8,128)(2,1)S(1)}, bf16[592,512]{1,0:T(8,128)(2,1)S(1)}, u32[]{:S(2)}, u32[]{:S(2)}) collective-permute-start(bf16[592,512]{1,0:T(8,128)(2,1)S(1)} %collective-permute-done.1.refs_2_), channel_id=1, source_target_pairs={{0,1},{1,2},{2,3},{3,0},{4,7},{5,4},{6,5},{7,6},{8,9},{9,10},{10,1... | collective-permute-start | bytes 1818632 | tf_op jit(solution)/shard_map/ppermute | solution.py:1111
  71.3 7.8 %collective-permute-start.16 = (bf16[3,256,128]{2,1,0:T(8,128)(2,1)S(1)}, bf16[3,256,128]{2,1,0:T(8,128)(2,1)S(1)}, u32[]{:S(2)}, u32[]{:S(2)}) collective-permute-start(bf16[3,256,128]{2,1,0:T(8,128)(2,1)S(1)} %get-tuple-element.173), channel_id=1, source_target_pairs={{0,8},{4,12},{8,0},{12,4},{16,24},{20,28},{24,16},{28,20},{1,9},{5... | collective-permute-start | bytes 589832 | tf_op jit(solution)/shard_map/ppermute | solution.py:1088
  72.0 10.9 %collective-permute-start.17 = (bf16[3,256,128]{2,1,0:T(8,128)(2,1)S(1)}, bf16[3,256,128]{2,1,0:T(8,128)(2,1)S(1)}, u32[]{:S(2)}, u32[]{:S(2)}) collective-permute-start(bf16[3,256,128]{2,1,0:T(8,128)(2,1)S(1)} %get-tuple-element.174), channel_id=1, source_target_pairs={{0,16},{4,20},{8,24},{12,28},{16,0},{20,4},{24,8},{28,12},{1,17},{... | collective-permute-start | bytes 589832 | tf_op jit(solution)/shard_map/ppermute | solution.py:1088
  72.0 10.9 %collective-permute-start.18 = (bf16[3,256,128]{2,1,0:T(8,128)(2,1)S(1)}, bf16[3,256,128]{2,1,0:T(8,128)(2,1)S(1)}, u32[]{:S(2)}, u32[]{:S(2)}) collective-permute-start(bf16[3,256,128]{2,1,0:T(8,128)(2,1)S(1)} %get-tuple-element.175), channel_id=1, source_target_pairs={{0,24},{4,28},{8,16},{12,20},{16,8},{20,12},{24,0},{28,4},{1,25},{... | collective-permute-start | bytes 589832 | tf_op jit(solution)/shard_map/ppermute | solution.py:1088
  74.8 12.3 %collective-permute-start.15 = (bf16[592,512]{1,0:T(8,128)(2,1)S(1)}, bf16[592,512]{1,0:T(8,128)(2,1)S(1)}, u32[]{:S(2)}, u32[]{:S(2)}) collective-permute-start(bf16[592,512]{1,0:T(8,128)(2,1)S(1)} %collective-permute-done.1.refs_2_), channel_id=1, source_target_pairs={{0,4},{4,0},{8,12},{12,8},{16,20},{20,16},{24,28},{28,24},{1,5},{5... | collective-permute-start | bytes 1818632 | tf_op jit(solution)/shard_map/ppermute | solution.py:1088
  83.5 22.1 %collective-permute-start.23 = (bf16[512,384]{1,0:T(8,128)(2,1)S(1)}, bf16[512,384]{1,0:T(8,128)(2,1)S(1)}, u32[]{:S(2)}, u32[]{:S(2)}) collective-permute-start(bf16[512,384]{1,0:T(8,128)(2,1)S(1)} %assemble.1.refs_5_.refs_4_), channel_id=1, source_target_pairs={{0,8},{4,12},{8,0},{12,4},{16,24},{20,28},{24,16},{28,20},{1,9},{5... | collective-permute-start | bytes 1179656 | tf_op jit(solution)/shard_map/ppermute | solution.py:1088
  84.9 20.7 %collective-permute-start.24 = (bf16[512,384]{1,0:T(8,128)(2,1)S(1)}, bf16[512,384]{1,0:T(8,128)(2,1)S(1)}, u32[]{:S(2)}, u32[]{:S(2)}) collective-permute-start(bf16[512,384]{1,0:T(8,128)(2,1)S(1)} %assemble.1.refs_5_.refs_4_), channel_id=1, source_target_pairs={{0,16},{4,20},{8,24},{12,28},{16,0},{20,4},{24,8},{28,12},{1,17},{... | collective-permute-start | bytes 1179656 | tf_op jit(solution)/shard_map/ppermute | solution.py:1088
  85.3 20.3 %collective-permute-start.25 = (bf16[512,384]{1,0:T(8,128)(2,1)S(1)}, bf16[512,384]{1,0:T(8,128)(2,1)S(1)}, u32[]{:S(2)}, u32[]{:S(2)}) collective-permute-start(bf16[512,384]{1,0:T(8,128)(2,1)S(1)} %assemble.1.refs_5_.refs_4_), channel_id=1, source_target_pairs={{0,24},{4,28},{8,16},{12,20},{16,8},{20,12},{24,0},{28,4},{1,25},{... | collective-permute-start | bytes 1179656 | tf_op jit(solution)/shard_map/ppermute | solution.py:1088
  109.9 7.7 %collective-permute-start.26 = (bf16[4,1,4,80,512]{4,3,2,1,0:T(8,128)(2,1)S(1)}, bf16[4,1,4,80,512]{4,3,2,1,0:T(8,128)(2,1)S(1)}, u32[]{:S(2)}, u32[]{:S(2)}) collective-permute-start(bf16[4,1,4,80,512]{4,3,2,1,0:T(8,128)(2,1)S(1)} %get-tuple-element.200), channel_id=1, source_target_pairs={{0,4},{4,0},{8,12},{12,8},{16,20},{20,16},{24,28},{28,24},{1,5},{5... | collective-permute-start | bytes 3932168 | tf_op jit(solution)/shard_map/ppermute | solution.py:1088
  110.0 9.7 %collective-permute-start.20 = (bf16[3,256,128]{2,1,0:T(8,128)(2,1)S(1)}, bf16[3,256,128]{2,1,0:T(8,128)(2,1)S(1)}, u32[]{:S(2)}, u32[]{:S(2)}) collective-permute-start(bf16[3,256,128]{2,1,0:T(8,128)(2,1)S(1)} %get-tuple-element.183), channel_id=1, source_target_pairs={{0,8},{4,12},{8,0},{12,4},{16,24},{20,28},{24,16},{28,20},{1,9},{5... | collective-permute-start | bytes 589832 | tf_op jit(solution)/shard_map/ppermute | solution.py:1088
  111.4 11.3 %collective-permute-start.21 = (bf16[3,256,128]{2,1,0:T(8,128)(2,1)S(1)}, bf16[3,256,128]{2,1,0:T(8,128)(2,1)S(1)}, u32[]{:S(2)}, u32[]{:S(2)}) collective-permute-start(bf16[3,256,128]{2,1,0:T(8,128)(2,1)S(1)} %get-tuple-element.184), channel_id=1, source_target_pairs={{0,16},{4,20},{8,24},{12,28},{16,0},{20,4},{24,8},{28,12},{1,17},{... | collective-permute-start | bytes 589832 | tf_op jit(solution)/shard_map/ppermute | solution.py:1088
  111.8 10.9 %collective-permute-start.22 = (bf16[3,256,128]{2,1,0:T(8,128)(2,1)S(1)}, bf16[3,256,128]{2,1,0:T(8,128)(2,1)S(1)}, u32[]{:S(2)}, u32[]{:S(2)}) collective-permute-start(bf16[3,256,128]{2,1,0:T(8,128)(2,1)S(1)} %get-tuple-element.185), channel_id=1, source_target_pairs={{0,24},{4,28},{8,16},{12,20},{16,8},{20,12},{24,0},{28,4},{1,25},{... | collective-permute-start | bytes 589832 | tf_op jit(solution)/shard_map/ppermute | solution.py:1088
  117.6 19.1 %collective-permute-start.30 = (bf16[4,1,4,72,512]{4,3,2,1,0:T(8,128)(2,1)S(1)}, bf16[4,1,4,72,512]{4,3,2,1,0:T(8,128)(2,1)S(1)}, u32[]{:S(2)}, u32[]{:S(2)}) collective-permute-start(bf16[4,1,4,72,512]{4,3,2,1,0:T(8,128)(2,1)S(1)} %get-tuple-element.208), channel_id=1, source_target_pairs={{0,4},{4,0},{8,12},{12,8},{16,20},{20,16},{24,28},{28,24},{1,5},{5... | collective-permute-start | bytes 3538952 | tf_op jit(solution)/shard_map/ppermute | solution.py:1088
  118.2 17.0 %collective-permute-start.27 = (bf16[1,4,80,512]{3,2,1,0:T(8,128)(2,1)S(1)}, bf16[1,4,80,512]{3,2,1,0:T(8,128)(2,1)S(1)}, u32[]{:S(2)}, u32[]{:S(2)}) collective-permute-start(bf16[1,4,80,512]{3,2,1,0:T(8,128)(2,1)S(1)} %get-tuple-element.202), channel_id=1, source_target_pairs={{0,8},{4,12},{8,0},{12,4},{16,24},{20,28},{24,16},{28,20},{1,9},{5... | collective-permute-start | bytes 983048 | tf_op jit(solution)/shard_map/ppermute | solution.py:1088
  119.7 17.0 %collective-permute-start.28 = (bf16[1,4,80,512]{3,2,1,0:T(8,128)(2,1)S(1)}, bf16[1,4,80,512]{3,2,1,0:T(8,128)(2,1)S(1)}, u32[]{:S(2)}, u32[]{:S(2)}) collective-permute-start(bf16[1,4,80,512]{3,2,1,0:T(8,128)(2,1)S(1)} %get-tuple-element.203), channel_id=1, source_target_pairs={{0,16},{4,20},{8,24},{12,28},{16,0},{20,4},{24,8},{28,12},{1,17},{... | collective-permute-start | bytes 983048 | tf_op jit(solution)/shard_map/ppermute | solution.py:1088
  122.7 14.0 %collective-permute-start.29 = (bf16[1,4,80,512]{3,2,1,0:T(8,128)(2,1)S(1)}, bf16[1,4,80,512]{3,2,1,0:T(8,128)(2,1)S(1)}, u32[]{:S(2)}, u32[]{:S(2)}) collective-permute-start(bf16[1,4,80,512]{3,2,1,0:T(8,128)(2,1)S(1)} %get-tuple-element.204), channel_id=1, source_target_pairs={{0,24},{4,28},{8,16},{12,20},{16,8},{20,12},{24,0},{28,4},{1,25},{... | collective-permute-start | bytes 983048 | tf_op jit(solution)/shard_map/ppermute | solution.py:1088
  135.2 19.5 %collective-permute-start.34 = (bf16[1,1024,256]{2,1,0:T(8,128)(2,1)S(1)}, bf16[1,1024,256]{2,1,0:T(8,128)(2,1)S(1)}, u32[]{:S(2)}, u32[]{:S(2)}) collective-permute-start(bf16[1,1024,256]{2,1,0:T(8,128)(2,1)S(1)} %get-tuple-element.219), channel_id=1, source_target_pairs={{0,4},{4,0},{8,12},{12,8},{16,20},{20,16},{24,28},{28,24},{1,5},{5... | collective-permute-start | bytes 1572872 | tf_op jit(solution)/shard_map/ppermute | solution.py:1088
  137.2 16.4 %collective-permute-start.31 = (bf16[1,4,72,512]{3,2,1,0:T(8,128)(2,1)S(1)}, bf16[1,4,72,512]{3,2,1,0:T(8,128)(2,1)S(1)}, u32[]{:S(2)}, u32[]{:S(2)}) collective-permute-start(bf16[1,4,72,512]{3,2,1,0:T(8,128)(2,1)S(1)} %get-tuple-element.210), channel_id=1, source_target_pairs={{0,8},{4,12},{8,0},{12,4},{16,24},{20,28},{24,16},{28,20},{1,9},{5... | collective-permute-start | bytes 884744 | tf_op jit(solution)/shard_map/ppermute | solution.py:1088
  137.9 15.7 %collective-permute-start.32 = (bf16[1,4,72,512]{3,2,1,0:T(8,128)(2,1)S(1)}, bf16[1,4,72,512]{3,2,1,0:T(8,128)(2,1)S(1)}, u32[]{:S(2)}, u32[]{:S(2)}) collective-permute-start(bf16[1,4,72,512]{3,2,1,0:T(8,128)(2,1)S(1)} %get-tuple-element.211), channel_id=1, source_target_pairs={{0,16},{4,20},{8,24},{12,28},{16,0},{20,4},{24,8},{28,12},{1,17},{... | collective-permute-start | bytes 884744 | tf_op jit(solution)/shard_map/ppermute | solution.py:1088
  139.4 14.3 %collective-permute-start.33 = (bf16[1,4,72,512]{3,2,1,0:T(8,128)(2,1)S(1)}, bf16[1,4,72,512]{3,2,1,0:T(8,128)(2,1)S(1)}, u32[]{:S(2)}, u32[]{:S(2)}) collective-permute-start(bf16[1,4,72,512]{3,2,1,0:T(8,128)(2,1)S(1)} %get-tuple-element.212), channel_id=1, source_target_pairs={{0,24},{4,28},{8,16},{12,20},{16,8},{20,12},{24,0},{28,4},{1,25},{... | collective-permute-start | bytes 884744 | tf_op jit(solution)/shard_map/ppermute | solution.py:1088
  154.6 24.8 %collective-permute-start.39 = (bf16[2,152,512]{2,1,0:T(8,128)(2,1)S(1)}, bf16[2,152,512]{2,1,0:T(8,128)(2,1)S(1)}, u32[]{:S(2)}, u32[]{:S(2)}) collective-permute-start(bf16[2,152,512]{2,1,0:T(8,128)(2,1)S(1)} %bitcast.39), channel_id=1, source_target_pairs={{0,1},{1,0},{2,3},{3,2},{4,5},{5,4},{6,7},{7,6},{8,9},{9,8},{10,11... | collective-permute-start | bytes 933896 | tf_op jit(solution)/shard_map/ppermute | solution.py:1222
  159.1 16.3 %collective-permute-start.36 = (bf16[2,256,384]{2,1,0:T(8,128)(2,1)S(1)}, bf16[2,256,384]{2,1,0:T(8,128)(2,1)S(1)}, u32[]{:S(2)}, u32[]{:S(2)}) collective-permute-start(bf16[2,256,384]{2,1,0:T(8,128)(2,1)S(1)} %get-tuple-element.228), channel_id=1, source_target_pairs={{0,8},{4,12},{8,0},{12,4},{16,24},{20,28},{24,16},{28,20},{1,9},{5... | collective-permute-start | bytes 1179656 | tf_op jit(solution)/shard_map/ppermute | solution.py:1088
  160.1 18.1 %collective-permute-start.37 = (bf16[2,256,384]{2,1,0:T(8,128)(2,1)S(1)}, bf16[2,256,384]{2,1,0:T(8,128)(2,1)S(1)}, u32[]{:S(2)}, u32[]{:S(2)}) collective-permute-start(bf16[2,256,384]{2,1,0:T(8,128)(2,1)S(1)} %get-tuple-element.229), channel_id=1, source_target_pairs={{0,16},{4,20},{8,24},{12,28},{16,0},{20,4},{24,8},{28,12},{1,17},{... | collective-permute-start | bytes 1179656 | tf_op jit(solution)/shard_map/ppermute | solution.py:1088
  161.3 18.1 %collective-permute-start.38 = (bf16[2,256,384]{2,1,0:T(8,128)(2,1)S(1)}, bf16[2,256,384]{2,1,0:T(8,128)(2,1)S(1)}, u32[]{:S(2)}, u32[]{:S(2)}) collective-permute-start(bf16[2,256,384]{2,1,0:T(8,128)(2,1)S(1)} %get-tuple-element.230), channel_id=1, source_target_pairs={{0,24},{4,28},{8,16},{12,20},{16,8},{20,12},{24,0},{28,4},{1,25},{... | collective-permute-start | bytes 1179656 | tf_op jit(solution)/shard_map/ppermute | solution.py:1088
  183.7 7.7 %collective-permute-start.41 = (bf16[1,256,384]{2,1,0:T(8,128)(2,1)S(1)}, bf16[1,256,384]{2,1,0:T(8,128)(2,1)S(1)}, u32[]{:S(2)}, u32[]{:S(2)}) collective-permute-start(bf16[1,256,384]{2,1,0:T(8,128)(2,1)S(1)} %get-tuple-element.236), channel_id=1, source_target_pairs={{0,8},{4,12},{8,0},{12,4},{16,24},{20,28},{24,16},{28,20},{1,9},{5... | collective-permute-start | bytes 589832 | tf_op jit(solution)/shard_map/ppermute | solution.py:1088
  184.9 7.6 %collective-permute-start.42 = (bf16[1,256,384]{2,1,0:T(8,128)(2,1)S(1)}, bf16[1,256,384]{2,1,0:T(8,128)(2,1)S(1)}, u32[]{:S(2)}, u32[]{:S(2)}) collective-permute-start(bf16[1,256,384]{2,1,0:T(8,128)(2,1)S(1)} %get-tuple-element.237), channel_id=1, source_target_pairs={{0,16},{4,20},{8,24},{12,28},{16,0},{20,4},{24,8},{28,12},{1,17},{... | collective-permute-start | bytes 589832 | tf_op jit(solution)/shard_map/ppermute | solution.py:1088
  186.1 6.4 %collective-permute-start.44 = (bf16[64,384]{1,0:T(8,128)(2,1)S(1)}, bf16[64,384]{1,0:T(8,128)(2,1)S(1)}, u32[]{:S(2)}, u32[]{:S(2)}) collective-permute-start(bf16[64,384]{1,0:T(8,128)(2,1)S(1)} %get-tuple-element.243), channel_id=1, source_target_pairs={{0,8},{4,12},{8,0},{12,4},{16,24},{20,28},{24,16},{28,20},{1,9},{5... | collective-permute-start | bytes 147464 | tf_op jit(solution)/shard_map/ppermute | solution.py:1088
  187.1 6.8 %collective-permute-start.45 = (bf16[64,384]{1,0:T(8,128)(2,1)S(1)}, bf16[64,384]{1,0:T(8,128)(2,1)S(1)}, u32[]{:S(2)}, u32[]{:S(2)}) collective-permute-start(bf16[64,384]{1,0:T(8,128)(2,1)S(1)} %get-tuple-element.244), channel_id=1, source_target_pairs={{0,16},{4,20},{8,24},{12,28},{16,0},{20,4},{24,8},{28,12},{1,17},{... | collective-permute-start | bytes 147464 | tf_op jit(solution)/shard_map/ppermute | solution.py:1088
  187.9 6.0 %collective-permute-start.46 = (bf16[64,384]{1,0:T(8,128)(2,1)S(1)}, bf16[64,384]{1,0:T(8,128)(2,1)S(1)}, u32[]{:S(2)}, u32[]{:S(2)}) collective-permute-start(bf16[64,384]{1,0:T(8,128)(2,1)S(1)} %get-tuple-element.245), channel_id=1, source_target_pairs={{0,24},{4,28},{8,16},{12,20},{16,8},{20,12},{24,0},{28,4},{1,25},{... | collective-permute-start | bytes 147464 | tf_op jit(solution)/shard_map/ppermute | solution.py:1088
  194.5 9.4 %collective-permute-start.47 = (bf16[48,512]{1,0:T(8,128)(2,1)S(1)}, bf16[48,512]{1,0:T(8,128)(2,1)S(1)}, u32[]{:S(2)}, u32[]{:S(2)}) collective-permute-start(bf16[48,512]{1,0:T(8,128)(2,1)S(1)} %get-tuple-element.250), channel_id=1, source_target_pairs={{0,1},{1,0},{2,3},{3,2},{4,5},{5,4},{6,7},{7,6},{8,9},{9,8},{10,11... | collective-permute-start | bytes 147464 | tf_op jit(solution)/shard_map/ppermute | solution.py:1222
  194.8 12.8 %collective-permute-start.48 = (bf16[200,512]{1,0:T(8,128)(2,1)S(1)}, bf16[200,512]{1,0:T(8,128)(2,1)S(1)}, u32[]{:S(2)}, u32[]{:S(2)}) collective-permute-start(bf16[200,512]{1,0:T(8,128)(2,1)S(1)} %get-tuple-element.251), channel_id=1, source_target_pairs={{0,2},{1,3},{2,0},{3,1},{4,6},{5,7},{6,4},{7,5},{8,10},{9,11},{10,... | collective-permute-start | bytes 614408 | tf_op jit(solution)/shard_map/ppermute | solution.py:1222
  197.4 6.9 %collective-permute-start.49 = (bf16[48,512]{1,0:T(8,128)(2,1)S(1)}, bf16[48,512]{1,0:T(8,128)(2,1)S(1)}, u32[]{:S(2)}, u32[]{:S(2)}) collective-permute-start(bf16[48,512]{1,0:T(8,128)(2,1)S(1)} %get-tuple-element.252), channel_id=1, source_target_pairs={{0,3},{1,2},{2,1},{3,0},{4,7},{5,6},{6,5},{7,4},{8,11},{9,10},{10,... | collective-permute-start | bytes 147464 | tf_op jit(solution)/shard_map/ppermute | solution.py:1222
  199.0 12.2 %collective-permute-start.50 = (bf16[1,256,384]{2,1,0:T(8,128)(2,1)S(1)}, bf16[1,256,384]{2,1,0:T(8,128)(2,1)S(1)}, u32[]{:S(2)}, u32[]{:S(2)}) collective-permute-start(bf16[1,256,384]{2,1,0:T(8,128)(2,1)S(1)} %get-tuple-element.255), channel_id=1, source_target_pairs={{0,24},{4,28},{8,16},{12,20},{16,8},{20,12},{24,0},{28,4},{1,25},{... | collective-permute-start | bytes 589832 | tf_op jit(solution)/shard_map/ppermute | solution.py:1088
  207.6 7.3 %collective-permute-start.51 = (bf16[200,512]{1,0:T(8,128)(2,1)S(1)}, bf16[200,512]{1,0:T(8,128)(2,1)S(1)}, u32[]{:S(2)}, u32[]{:S(2)}) collective-permute-start(bf16[200,512]{1,0:T(8,128)(2,1)S(1)} %total.1.refs_0_), channel_id=1, source_target_pairs={{0,8},{4,12},{8,0},{12,4},{16,24},{20,28},{24,16},{28,20},{1,9},{5... | collective-permute-start | bytes 614408 | tf_op jit(solution)/shard_map/ppermute | solution.py:1088
  208.8 9.2 %collective-permute-start.52 = (bf16[200,512]{1,0:T(8,128)(2,1)S(1)}, bf16[200,512]{1,0:T(8,128)(2,1)S(1)}, u32[]{:S(2)}, u32[]{:S(2)}) collective-permute-start(bf16[200,512]{1,0:T(8,128)(2,1)S(1)} %total.1.refs_0_), channel_id=1, source_target_pairs={{0,16},{4,20},{8,24},{12,28},{16,0},{20,4},{24,8},{28,12},{1,17},{... | collective-permute-start | bytes 614408 | tf_op jit(solution)/shard_map/ppermute | solution.py:1088
  209.6 8.3 %collective-permute-start.53 = (bf16[200,512]{1,0:T(8,128)(2,1)S(1)}, bf16[200,512]{1,0:T(8,128)(2,1)S(1)}, u32[]{:S(2)}, u32[]{:S(2)}) collective-permute-start(bf16[200,512]{1,0:T(8,128)(2,1)S(1)} %total.1.refs_0_), channel_id=1, source_target_pairs={{0,24},{4,28},{8,16},{12,20},{16,8},{20,12},{24,0},{28,4},{1,25},{... | collective-permute-start | bytes 614408 | tf_op jit(solution)/shard_map/ppermute | solution.py:1088
  213.8 5.3 %collective-permute-start.54 = (bf16[200,512]{1,0:T(8,128)(2,1)S(1)}, bf16[200,512]{1,0:T(8,128)(2,1)S(1)}, u32[]{:S(2)}, u32[]{:S(2)}) collective-permute-start(bf16[200,512]{1,0:T(8,128)(2,1)S(1)} %total.1.refs_0_), channel_id=1, source_target_pairs={{0,4},{4,0},{8,12},{12,8},{16,20},{20,16},{24,28},{28,24},{1,5},{5... | collective-permute-start | bytes 614408 | tf_op jit(solution)/shard_map/ppermute | solution.py:1088
  (31 other events, 218.3 us)
where the time goes:
time: 231 us; the launch traced here: 226 us
  Pallas kernels  108 us (47%)
  starting transfers between devices  55.8 us (24%)
  waiting for transfers between devices  51.3 us (22%)
  local copies, waits for them, and re-layouts  5.33 us (2%)
  between operations  4.64 us (2%)
    ppermute x49, starting transfers between devices, swap(): return lax.ppermute(x, 'ctx', [(i, i ^ distance) for i in range(ctx)])  42.6 us
    pallas_call x3, Pallas kernels, attend_back(): pl.pallas_call(functools.partial(attend_back_kernel, len(kvs)), grid=(1,)...  38 us
    ppermute x49, waiting for transfers between devices, swap(): return lax.ppermute(x, 'ctx', [(i, i ^ distance) for i in range(ctx)])  32.7 us
    pallas_call x3, Pallas kernels, attend(): pl.pallas_call(functools.partial(attend_kernel, len(kvs), carried), grid=...  18.9 us
    pallas_call x1, Pallas kernels, dense(): pl.pallas_call(dense_kernel, grid=(seqs,), in_specs=[scalars, scalars] +...  18.5 us
    ppermute x3, waiting for transfers between devices, body(): turn = lambda x: lax.ppermute(x, ('ctx', 'wsh'), ring)  8.79 us
    pallas_call x2, Pallas kernels, split_grads(): pl.pallas_call(kernel, grid_spec=pltpu.PrefetchScalarGridSpec(num_scalar_...  8.26 us
    ppermute x2, waiting for transfers between devices, body(): lax.ppermute(x, ('ctx', 'wsh'), [(c * wsh + (pair_of(c) ^ z), c * wsh + (...  6.14 us
  transfers between devices with their start and end apart: 58, of which 25 were waited for; matrix products, arithmetic and copies ran while one was open for 1% of the time, Pallas kernels for 41%

commit v1 on v0

--- a/solution.py
+++ b/solution.py
@@ -114,32 +114,52 @@
 
     @pl.when(flag_ref[0] != 1)
     def _():
-        outs, masses = [], []
-        for head in range(2):
-            mine = masked(head)
-            fold = (
-                jnp.zeros((step, WIDE), f32),
-                jnp.full((step, 1), -jnp.inf, f32),
-                jnp.zeros((step, 1), f32),
-            )
-            for ref in kv_refs:
-
-                def body(i, fold, ref=ref, mine=mine):
-                    weighted, top, total = fold
-                    at = pl.ds(pl.multiple_of(i * size, size), size)
-                    scores = dot(mine, ref[0, at, :WIDE], NT) * scale
-                    now = jnp.maximum(top, jnp.max(scores, axis=1, keepdims=True))
-                    factor = jnp.exp2(top - now)
-                    e = jnp.exp2(scores - now)
-                    total = total * factor + jnp.sum(e, axis=1, keepdims=True)
-                    weighted = weighted * factor + dot(e.astype(bf16), ref[0, at, WIDE:])
-                    return weighted, now, total
-
-                fold = lax.fori_loop(0, ref.shape[1] // size, body, fold)
-            weighted, top, total = fold
-            outs.append(weighted * (1.0 / total))
-            masses.append(top + jnp.log2(total))
-        finish(outs, masses)
+        some = 128
+        left = lane_masks((some, WIDE))
+        block = low_refs[0].shape[1]
+
+        def rows_body(r, carry):
+            start = pl.multiple_of(r * some, some)
+            x = q_ref[0, pl.ds(pl.multiple_of(index * step + start, some), some)]
+            outs, masses = [], []
+            for head in range(2):
+                mine = jnp.where(left == (head == 0), x, jnp.zeros_like(x))
+                fold = (
+                    jnp.zeros((some, WIDE), f32),
+                    jnp.full((some, 1), -jnp.inf, f32),
+                    jnp.zeros((some, 1), f32),
+                )
+                for ref in kv_refs:
+
+                    def body(i, fold, ref=ref, mine=mine):
+                        weighted, top, total = fold
+                        at = pl.ds(pl.multiple_of(i * size, size), size)
+                        scores = dot(mine, ref[0, at, :WIDE], NT) * scale
+                        now = jnp.maximum(top, jnp.max(scores, axis=1, keepdims=True))
+                        factor = jnp.exp2(top - now)
+                        e = jnp.exp2(scores - now)
+                        total = total * factor + jnp.sum(e, axis=1, keepdims=True)
+                        weighted = weighted * factor + dot(e.astype(bf16), ref[0, at, WIDE:])
+                        return weighted, now, total
+
+                    fold = lax.fori_loop(0, ref.shape[1] // size, body, fold)
+                weighted, top, total = fold
+                outs.append(weighted * (1.0 / total))
+                masses.append(top + jnp.log2(total))
+            out = jnp.where(left, outs[0], outs[1])
+            o_ref[0, pl.ds(start, some)] = out
+            low = out.astype(bf16)
+            for d, ref in enumerate(low_refs):
+
+                @pl.when((index * step + start) // block == d)
+                def _(ref=ref):
+                    ref[0, pl.ds(pl.multiple_of(lax.rem(start, block), some), some)] = low
+
+            turned = jnp.transpose(jnp.where(left, masses[0], masses[1]))
+            mass_ref[0, :, pl.ds(start, some)] = jnp.concatenate([turned[0:4], turned[64:68]], axis=0)
+            return carry
+
+        lax.fori_loop(0, step // some, rows_body, 0)
 
 
 def attend(at, seqs, q, kvs, before):
@@ -615,7 +635,7 @@
         ),
         out_shape=[jax.ShapeDtypeStruct(shape, bf16)] * 2,
         compiler_params=room(24),
-        cost_estimate=cost(4.5),
+        cost_estimate=cost(1),
         name=name,
     )(info, *arrays)
 
@@ -822,11 +842,11 @@
     att_refs, refs = refs[:PAIRS], refs[PAIRS:]
     emb_ref, prev_ref, gt_ref, gb_ref, hsum_ref, code_ref, gsum_ref = refs[:7]
     refs = refs[7:]
-    final_ref, blend_ref, rows_ref, gprev_ref, base_ref = refs[:5]
-    gatt_refs = refs[5:9]
-    nlow_ref, ilow_ref, gin_ref, gfeed_ref, gbranch_ref, vsum_ref, bsum_ref = refs[9:16]
-    slope_ref, win_ref, wouter_ref, wout_ref, small_ref, sem = refs[16:22]
-    buffers, row_sem = refs[22:26], refs[26]
+    final_ref, blend_ref, nsum_ref, ghalt_ref, gprev_ref, base_ref = refs[:6]
+    gatt_refs = refs[6:10]
+    nlow_ref, ilow_ref, gin_ref, gfeed_ref, gbranch_ref, vsum_ref, bsum_ref = refs[10:17]
+    slope_ref, win_ref, wouter_ref, wout_ref, small_ref, sem = refs[17:23]
+    buffers, row_sem = refs[23:27], refs[27]
     me = pl.program_id(0)
 
     def fetch(step):
@@ -887,9 +907,9 @@
         jnp.concatenate([small_ref[a, i + 1 : i + 2, :WIDE] for a in range(PAIRS)], axis=1).astype(f32)
         for i in range(6)
     ]
-    at = pl.ds(pl.program_id(0), 1)
+    at_row = pl.ds(pl.program_id(0), 1)
     row = lax.broadcasted_iota(jnp.int32, (8, emb.shape[0]), 0)
-    lines = jnp.where(row == 0, hsum_ref[at], jnp.where(row == 1, code_ref[at].astype(f32), gsum_ref[at]))
+    lines = jnp.where(row == 0, hsum_ref[at_row], jnp.where(row == 1, code_ref[at_row].astype(f32), gsum_ref[at_row]))
     cols = jnp.transpose(lines)
     sum_col, code_col, gsum_col = cols[:, 0:1], cols[:, 1:2], cols[:, 2:3]
     z1 = emb + dot(att, w_out)
@@ -922,7 +942,9 @@
     g_logit = g_update * running * (1.0 - halting) * halt_prob * (1.0 - halt_prob)
     lane = lax.broadcasted_iota(jnp.int32, (emb.shape[0], WIDE), 1)
     packed = jnp.where(lane == 0, sum_col + update, jnp.where(lane == 1, g_halt_sum, 0.0))
-    rows_ref[0] = jnp.transpose(packed)[0:8]
+    turned = jnp.transpose(packed)
+    nsum_ref[at_row] = turned[0:1]
+    ghalt_ref[at_row] = turned[1:2]
     gf = gt.astype(f32) + update * gb
     g_two = norm_back(gf, n2, i2, g2)
     gfeed = g_two.astype(bf16)
@@ -978,7 +1000,8 @@
         out_specs=[
             rowspec(width),
             rowspec(width),
-            pl.BlockSpec((1, 8, rows), lambda s: (s, 0, 0)),
+            pl.BlockSpec((seqs, rows), lambda s: (0, 0)),
+            pl.BlockSpec((seqs, rows), lambda s: (0, 0)),
             rowspec(width),
             rowspec(width),
             rowspec(WIDE),
@@ -996,7 +1019,8 @@
         out_shape=[
             shape(width, bf16),
             shape(width, bf16),
-            jax.ShapeDtypeStruct((seqs, 8, rows), f32),
+            jax.ShapeDtypeStruct((seqs, rows), f32),
+            jax.ShapeDtypeStruct((seqs, rows), f32),
             shape(width, f32),
             shape(width, f32),
             shape(WIDE, bf16),
@@ -1128,7 +1152,8 @@
     vectors = [b_outer, gain_attention, shift_attention, gain_feedforward, shift_feedforward, w_halt]
     feed = pack_feed(after(info, held), w_inner, w_outer, w_out, b_inner, vectors)
     feed_mine = [feed, turn(feed)]
-    chosen = choose(after(info, feed_mine[1], *tokens[1:3]), near, far)
+    feed_first = sibling(feed)
+    chosen = choose(after(info, feed_mine[1], feed_first, *tokens[1:3]), near, far)
     w_mine = assemble(info, chosen, sibling(chosen))
 
     groups = [[r * 2 * PAIRS + i for r in range(repeats)] for i in range(2 * PAIRS)]
@@ -1153,7 +1178,7 @@
     fold = attend(0, seqs, q_list[0], kvs_list[0], None)
     feed_mine.append(turn(after(feed_mine[2], fold[1])))
     fold = attend(1, seqs, after(q_list[1], feed_mine[2], kvs_list[2][-1]), kvs_list[1], fold)
-    feed_other = [sibling(after(x, fold[1])) for x in feed_mine[:2]]
+    feed_other = [feed_first, sibling(after(feed_mine[1], fold[1]))]
     fold = attend(2, seqs, after(q_list[2], *feed_other), kvs_list[2], fold)
     o32, mass, *low = fold
     att = [low[0]] + [partners(low[d], d) for d in range(1, PAIRS)]
@@ -1164,7 +1189,8 @@
     (
         final,
         blended,
-        row_out,
+        new_sum,
+        grad_halt_sum,
         grad_prev,
         base,
         gatt0,
@@ -1182,8 +1208,6 @@
         info, b_halt.reshape(1, 1), feed_mine, feed_other, emb, att, prev_state, grad_transformed, grad_blended,
         [halt_sum, halt_code, grad_sum], part, out_rows,
     )
-    new_sum = row_out[:, 0]
-    grad_halt_sum = row_out[:, 1]
     gs = [gatt0] + [partners(x, d + 1) for d, x in enumerate((gatt1, gatt2, gatt3))]
 
     keep_a, give_a = outer_grads(after(info, vsum, *w_order[1:]), att, ilow, gfeed, gbranch, ctx)
@@ -1229,20 +1253,21 @@
     own, sent = halve(after(share_keep[0], backs[2][0], *blocks[1:]), moved)
     made = combine(info, (2,), tokens, [got(backs[2], own)], gq, repeats == 1)
     pieces, keep, give = made[:PAIRS], made[PAIRS], made[-1]
-    block = [pieces[0]] + [partners(pieces[d], d) for d in (1, 2)]
     if repeats == 1:
-        heads = share_small(after(info, *block), sent, spread_pieces(join_small(keep, sibling(give))))
-        block.append(partners(after(pieces[3], heads[0]), 3))
+        small = join_small(keep, sibling(give))
+        block = [pieces[0]] + [partners(after(pieces[d], small[0]), d) for d in (1, 2)]
+        heads = share_small(info, sent, spread_pieces(small))
         heads = [heads[0]] + [cross(heads[step], step) for step in range(1, wsh)]
         grad_state = add_state(0, after(base, heads[0]), blocks, w_order)
-        share = total_parts(after(own, grad_state), heads)
+        share = total_parts(after(own, grad_state, *block[1:]), heads)
+        block.append(partners(after(pieces[3], grad_state), 3))
         grad_state = add_state(2, after(grad_state, share), block, w_order)
         mine = spread_pieces([share] * PAIRS)
         (grad_w_outer, grad_w_out, grad_w_inner, tail, grad_w_query, grad_w_key, grad_w_value) = unpack(
             info, mine, [sibling(after(x, grad_state)) for x in mine], part, out_rows
         )
     else:
-        block.append(partners(pieces[3], 3))
+        block = spread_pieces(pieces)
         share = total_parts(own, [cross(sent, 2)])
         grad_state = add_state(2, add_state(0, base, blocks, w_order), block, w_order)
         whole = lax.all_gather(share, "ctx", axis=0).astype(f32)

time: 231 us -> 227 us (0.983)
    ppermute x49, waiting for transfers between devices: 32.7 us -> 29.3 us  [swap(): return lax.ppermute(x, 'ctx', [(i, i ^ distance) for i in range(ctx)])]
  transfers between devices with their start and end apart: 58 -> 58, of which waited for: 25 -> 23; matrix products, arithmetic and copies ran while one was open for 1% -> 1% of each run, Pallas kernels for 41% -> 41%
where the time goes in v1:
time: 227 us; the launch traced here: 224 us
  Pallas kernels  107 us (47%)
  starting transfers between devices  55.7 us (25%)
  waiting for transfers between devices  50 us (22%)
  local copies, waits for them, and re-layouts  4.67 us (2%)
  between operations  4.67 us (2%)
    ppermute x49, starting transfers between devices, swap(): return lax.ppermute(x, 'ctx', [(i, i ^ distance) for i in range(ctx)])  41.6 us
    pallas_call x3, Pallas kernels, attend_back(): pl.pallas_call(functools.partial(attend_back_kernel, len(kvs)), grid=(1,)...  38.3 us
    ppermute x49, waiting for transfers between devices, swap(): return lax.ppermute(x, 'ctx', [(i, i ^ distance) for i in range(ctx)])  29.3 us
    pallas_call x3, Pallas kernels, attend(): pl.pallas_call(functools.partial(attend_kernel, len(kvs), carried), grid=...  18.4 us
    pallas_call x1, Pallas kernels, dense(): pl.pallas_call(dense_kernel, grid=(seqs,), in_specs=[scalars, scalars] +...  18.3 us
    ppermute x3, waiting for transfers between devices, body(): turn = lambda x: lax.ppermute(x, ('ctx', 'wsh'), ring)  10.8 us
    pallas_call x2, Pallas kernels, split_grads(): pl.pallas_call(kernel, grid_spec=pltpu.PrefetchScalarGridSpec(num_scalar_...  8.03 us
    ppermute x2, waiting for transfers between devices, body(): lax.ppermute(x, ('ctx', 'wsh'), [(c * wsh + (pair_of(c) ^ z), c * wsh + (...  6.14 us
  transfers between devices with their start and end apart: 58, of which 23 were waited for; matrix products, arithmetic and copies ran while one was open for 1% of the time, Pallas kernels for 41%

profile of v1, /device:TPU:0, one launch (start us, length us, event | category | flops | bytes accessed | tf_op | source)
XLA Modules:
  0.0 223.8 jit_solution(6425080344880796768)
XLA Ops:
  2.5 3.0 %collective-permute-start.2 = (bf16[3,256,512]{2,1,0:T(8,128)(2,1)S(1)}, bf16[3,256,512]{2,1,0:T(8,128)(2,1)S(1)}, u32[]{:S(2)}, u32[]{:S(2)}) collective-permute-start(bf16[3,256,512]{2,1,0:T(8,128)(2,1)S(1)} %get-tuple-element.271.refs_0_), channel_id=1, source_target_pairs={{0,8},{4,12},{8,0},{12,4},{16,24},{20,28},{24,16},{28,20},{1,9},{5... | collective-permute-start | bytes 2359304 | tf_op jit(solution)/shard_map/ppermute | solution.py:1112
  5.5 1.5 collective-permute-start.3
  9.6 3.5 %collective-permute-start.7 = (bf16[256,384]{1,0:T(8,128)(2,1)S(1)}, bf16[256,384]{1,0:T(8,128)(2,1)S(1)}, u32[]{:S(2)}, u32[]{:S(2)}) collective-permute-start(bf16[256,384]{1,0:T(8,128)(2,1)S(1)} %pack.1), channel_id=1, source_target_pairs={{0,1},{4,5},{9,8},{13,12},{18,19},{22,23},{27,26},{31,30}} | collective-permute-start | bytes 589832 | tf_op jit(solution)/shard_map/ppermute | solution.py:1143
  14.7 3.7 %collective-permute-done.7 = bf16[256,384]{1,0:T(8,128)(2,1)S(1)} collective-permute-done((bf16[256,384]{1,0:T(8,128)(2,1)S(1)}, bf16[256,384]{1,0:T(8,128)(2,1)S(1)}, u32[]{:S(2)}, u32[]{:S(2)}) %collective-permute-start.7) | collective-permute-done | bytes 196640 | tf_op jit(solution)/shard_map/ppermute | solution.py:1143
  19.7 4.9 %collective-permute-done.3.refs_2_ = bf16[3,256,512]{2,1,0:T(8,128)(2,1)} collective-permute-done((bf16[3,256,512]{2,1,0:T(8,128)(2,1)S(1)}, bf16[3,256,512]{2,1,0:T(8,128)(2,1)}, u32[]{:S(2)}, u32[]{:S(2)}) %collective-permute-start.3) | collective-permute-done | bytes 786464 | tf_op jit(solution)/shard_map/ppermute | solution.py:1112
  26.1 1.8 collective-permute-start.5
  27.9 3.6 %collective-permute-done.refs_1_ = bf16[592,512]{1,0:T(8,128)(2,1)} collective-permute-done((bf16[592,512]{1,0:T(8,128)(2,1)}, bf16[592,512]{1,0:T(8,128)(2,1)}, u32[]{:S(2)}, u32[]{:S(2)}) %collective-permute-start) | collective-permute-done | bytes 606240 | tf_op jit(solution)/shard_map/ppermute | solution.py:1135
  31.5 2.4 %collective-permute-done.8.far_ref = bf16[256,384]{1,0:T(8,128)(2,1)S(1)} collective-permute-done((bf16[256,384]{1,0:T(8,128)(2,1)S(1)}, bf16[256,384]{1,0:T(8,128)(2,1)S(1)}, u32[]{:S(2)}, u32[]{:S(2)}) %collective-permute-start.8) | collective-permute-done | bytes 196640 | tf_op jit(solution)/shard_map/ppermute | solution.py:1143
  34.5 4.1 %collective-permute-start.1 = (bf16[592,512]{1,0:T(8,128)(2,1)}, bf16[592,512]{1,0:T(8,128)(2,1)S(1)}, u32[]{:S(2)}, u32[]{:S(2)}) collective-permute-start(bf16[592,512]{1,0:T(8,128)(2,1)} %collective-permute-done.refs_1_), channel_id=1, source_target_pairs={{0,1},{1,2},{2,3},{3,0},{4,7},{5,4},{6,5},{7,6},{8,9},{9,10},{10,1... | collective-permute-start | bytes 1818632 | tf_op jit(solution)/shard_map/ppermute | solution.py:1135
  39.3 1.6 project.3
  41.0 3.0 %collective-permute-start.10 = (bf16[1,1024,256]{2,1,0:T(8,128)(2,1)S(1)}, bf16[1,1024,256]{2,1,0:T(8,128)(2,1)S(1)}, u32[]{:S(2)}, u32[]{:S(2)}) collective-permute-start(bf16[1,1024,256]{2,1,0:T(8,128)(2,1)S(1)} %get-tuple-element.148.refs_0_.refs_6_), channel_id=1, source_target_pairs={{0,4},{4,0},{8,12},{12,8},{16,20},{20,16},{24,28},{28,24},{1,5},{5... | collective-permute-start | bytes 1572872 | tf_op jit(solution)/shard_map/ppermute | solution.py:1112
  44.0 1.6 project.4
  45.6 1.7 project.5
  47.9 6.1 %attend.3 = (f32[3,1024,128]{2,1,0:T(8,128)S(1)}, f32[3,8,1024]{2,1,0:T(8,128)S(1)}, bf16[3,256,128]{2,1,0:T(8,128)(2,1)S(1)}, bf16[3,256,128]{2,1,0:T(8,128)(2,...) custom-call(bf16[1,1024,128]{2,1,0:T(8,128)(2,1)S(1)} %get-tuple-element.147.q_ref, ...), custom_call_target="tpu_custom_call" | custom-call | flops 1100000000 | bytes 1024 | tf_op jit(solution)/shard_map/attend/pallas_call | solution.py:175
  54.0 2.0 collective-permute-done.1.refs_2_
  56.0 6.1 %attend.4 = (f32[3,1024,128]{2,1,0:T(8,128)S(1)}, f32[3,8,1024]{2,1,0:T(8,128)S(1)}, bf16[3,256,128]{2,1,0:T(8,128)(2,1)S(1)}, bf16[3,256,128]{2,1,0:T(8,128)(2,...) custom-call(bf16[1,1024,128]{2,1,0:T(8,128)(2,1)S(1)} %get-tuple-ele, ...), custom_call_target="tpu_custom_call", output_to_operand_aliasing={{0}: (3, {}), {1}: (4, {}), {2}: (5, {}), {3}: (6, {}), {4}... | custom-call | flops 1100000000 | bytes 1024 | tf_op jit(solution)/shard_map/attend/pallas_call | solution.py:175
  62.8 1.6 collective-permute-done.14.refs_5_
  64.5 6.1 %attend.5 = (f32[3,1024,128]{2,1,0:T(8,128)S(1)}, f32[3,8,1024]{2,1,0:T(8,128)S(1)}, bf16[3,256,128]{2,1,0:T(8,128)(2,1)S(1)}, bf16[3,256,128]{2,1,0:T(8,128)(2,...) custom-call(bf16[1,1024,128]{2,1,0:T(8,128)(2,1)S(1)} %get-tuple-ele, ...), custom_call_target="tpu_custom_call", output_to_operand_aliasing={{0}: (3, {}), {1}: (4, {}), {2}: (5, {}), {3}: (6, {}), {4}... | custom-call | flops 1100000000 | bytes 1024 | tf_op jit(solution)/shard_map/attend/pallas_call | solution.py:175
  71.3 2.8 %collective-permute-start.18 = (bf16[3,256,128]{2,1,0:T(8,128)(2,1)S(1)}, bf16[3,256,128]{2,1,0:T(8,128)(2,1)S(1)}, u32[]{:S(2)}, u32[]{:S(2)}) collective-permute-start(bf16[3,256,128]{2,1,0:T(8,128)(2,1)S(1)} %get-tuple-element.175), channel_id=1, source_target_pairs={{0,24},{4,28},{8,16},{12,20},{16,8},{20,12},{24,0},{28,4},{1,25},{... | collective-permute-start | bytes 589832 | tf_op jit(solution)/shard_map/ppermute | solution.py:1112
  74.1 5.2 %collective-permute-done.11.refs_3_ = bf16[592,512]{1,0:T(8,128)(2,1)S(1)} collective-permute-done((bf16[592,512]{1,0:T(8,128)(2,1)S(1)}, bf16[592,512]{1,0:T(8,128)(2,1)S(1)}, u32[]{:S(2)}, u32[]{:S(2)}) %collective-permute-start.11) | collective-permute-done | bytes 606240 | tf_op jit(solution)/shard_map/ppermute | solution.py:1135
  79.3 3.5 %collective-permute-done.17.refs_10_.a2_ref = bf16[3,256,128]{2,1,0:T(8,128)(2,1)S(1)} collective-permute-done((bf16[3,256,128]{2,1,0:T(8,128)(2,1)S(1)}, bf16[3,256,128]{2,1,0:T(8,128)(2,1)S(1)}, u32[]{:S(2)}, u32[]{:S(2)}) %collective-permute-start.17) | collective-permute-done | bytes 196640 | tf_op jit(solution)/shard_map/ppermute | solution.py:1112
  85.3 1.8 collective-permute-start.25
  87.1 18.3 %dense.1 = (bf16[3,256,512]{2,1,0:T(8,128)(2,1)}, bf16[3,256,512]{2,1,0:T(8,128)(2,1)}, f32[3,256]{1,0:T(4,128)}, f32[3,256]{1,0:T(4,128)}, f32[3,256,512]{2,1,0...) custom-call(s32[3]{0:T(128)S(1)} %pad_add_fusion.info_ref, ...), custom_call_target="tpu_custom_call" | custom-call | flops 22000001024 | bytes 1024 | tf_op jit(solution)/shard_map/dense/pallas_call | solution.py:992
  105.5 4.2 %outer_grads.1 = (bf16[4,1,4,80,512]{4,3,2,1,0:T(8,128)(2,1)S(1)}, bf16[4,1,4,80,512]{4,3,2,1,0:T(8,128)(2,1)S(1)}) custom-call(s32[3]{0:T(128)S(1)} %pad_add_fusion.info_ref, bf16[3,256,128]{2,1,0:T(8,128)(2,1)S(1)} %get-tuple-element.177.refs_8_.a0_ref, bf16[3,256,128]{2,1,0:T(8,128)(2,1)S(1)} %collective-permute-done.16.refs_9_.a1_ref, ...), custom_call_target="tpu_custom_call" | custom-call | flops 1100000000 | bytes 1024 | tf_op jit(solution)/shard_map/outer_grads/pallas_call | solution.py:631
  109.8 1.4 collective-permute-start.20
  111.6 1.7 collective-permute-start.22
  113.4 3.8 %inner_grads.1 = (bf16[4,1,4,72,512]{4,3,2,1,0:T(8,128)(2,1)S(1)}, bf16[4,1,4,72,512]{4,3,2,1,0:T(8,128)(2,1)S(1)}) custom-call(s32[3]{0:T(128)S(1)} %pad_add_fusion.info_ref, bf16[3,256,512]{2,1,0:T(8,128)(2,1)S(1)} %get-tuple-element.195.nlow_ref, bf16[3,256,2048]{2,1,0:T(8,128)(2,1)S(1)} %copy-done.18, f32[3,8,512]{2,1,0:T(8,128)S(1)} %get-tuple-element.187.vsum_ref, ...), custom_call_target="tpu_custom_call" | custom-call | flops 1100000000 | bytes 1024 | tf_op jit(solution)/shard_map/inner_grads/pallas_call | solution.py:631
  119.7 3.0 %collective-permute-done.21.refs_2_ = bf16[3,256,128]{2,1,0:T(8,128)(2,1)S(1)} collective-permute-done((bf16[3,256,128]{2,1,0:T(8,128)(2,1)S(1)}, bf16[3,256,128]{2,1,0:T(8,128)(2,1)S(1)}, u32[]{:S(2)}, u32[]{:S(2)}) %collective-permute-start.21) | collective-permute-done | bytes 196640 | tf_op jit(solution)/shard_map/ppermute | solution.py:1112
  122.6 12.7 %attend_back.3 = (bf16[1,1024,128]{2,1,0:T(8,128)(2,1)S(1)}, f32[1,1024,256]{2,1,0:T(8,128)S(1)}, bf16[1,1024,256]{2,1,0:T(8,128)(2,1)S(1)}) custom-call(bf16[1,1024,128]{2,1,0:T(8,128)(2,1)S(1)} %get-tuple-element.147.q_ref, bf16[3,256,128]{2,1,0:T(8,128)(2,1)S(1)} %get-tuple-element.182.refs_0_, bf16[3,256,128]{2,1,0:T(8,128)(2,1)S(1)} %collective-permute-done.20.refs_1_, ...), custom_call_target="tpu_custom_call" | custom-call | flops 15399999488 | bytes 1024 | tf_op jit(solution)/shard_map/attend_back/pallas_call | solution.py:257
  137.8 1.8 collective-permute-start.32
  140.6 12.8 %attend_back.4 = (bf16[1,1024,128]{2,1,0:T(8,128)(2,1)S(1)}, f32[1,1024,256]{2,1,0:T(8,128)S(1)}, bf16[1,1024,256]{2,1,0:T(8,128)(2,1)S(1)}) custom-call(bf16[1,1024,128]{2,1,0:T(8,128)(2,1)S(1)} %get-tuple-element.155.q_ref, bf16[3,256,128]{2,1,0:T(8,128)(2,1)S(1)} %get-tuple-element.182.refs_0_, bf16[3,256,128]{2,1,0:T(8,128)(2,1)S(1)} %collective-permute-done.20.refs_1_, ...), custom_call_target="tpu_custom_call" | custom-call | flops 15399999488 | bytes 1024 | tf_op jit(solution)/shard_map/attend_back/pallas_call | solution.py:257
  154.5 1.8 collective-permute-done.35.refs_10_
  156.3 2.6 %combine.2 = (bf16[2,256,384]{2,1,0:T(8,128)(2,1)S(1)}, bf16[2,256,384]{2,1,0:T(8,128)(2,1)S(1)}, bf16[2,256,384]{2,1,0:T(8,128)(2,1)S(1)}, bf16[2,256,384]{2,1,0:T(8,128)(2,1)S(1)}, f32[512,384]{1,0:T(8,128)S(1)}) custom-call(s32[3]{0:T(128)S(1)} %pad_add_fusion.info_ref, bf16[3,256,512]{2,1,0:T(8,128)(2,1)S(1)} %get-tuple-element.271.refs_0_, ...), custom_call_target="tpu_custom_call" | custom-call | flops 2200000000 | bytes 1024 | tf_op jit(solution)/shard_map/combine/pallas_call | solution.py:430
  162.5 12.8 %attend_back.5 = (bf16[1,1024,128]{2,1,0:T(8,128)(2,1)S(1)}, f32[1,1024,256]{2,1,0:T(8,128)S(1)}, bf16[1,1024,256]{2,1,0:T(8,128)(2,1)S(1)}) custom-call(bf16[1,1024,128]{2,1,0:T(8,128)(2,1)S(1)} %get-tuple-element.165.q_ref, bf16[3,256,128]{2,1,0:T(8,128)(2,1)S(1)} %get-tuple-element.182.refs_0_, bf16[3,256,128]{2,1,0:T(8,128)(2,1)S(1)} %collective-permute-done.20.refs_1_, ...), custom_call_target="tpu_custom_call" | custom-call | flops 15399999488 | bytes 1024 | tf_op jit(solution)/shard_map/attend_back/pallas_call | solution.py:257
  175.3 3.0 %collective-permute-done.37.refs_2_ = bf16[2,256,384]{2,1,0:T(8,128)(2,1)S(1)} collective-permute-done((bf16[2,256,384]{2,1,0:T(8,128)(2,1)S(1)}, bf16[2,256,384]{2,1,0:T(8,128)(2,1)S(1)}, u32[]{:S(2)}, u32[]{:S(2)}) %collective-permute-start.37) | collective-permute-done | bytes 393248 | tf_op jit(solution)/shard_map/ppermute | solution.py:1112
  179.8 1.9 collective-permute-done.40.refs_7_
  181.7 2.1 combine.3
  186.2 1.4 collective-permute-start.43
  189.7 1.4 collective-permute-start.46
  191.2 2.0 collective-permute-done.44.refs_3_
  194.2 3.3 %add_state.2.base_ref = f32[3,256,512]{2,1,0:T(8,128)} custom-call(f32[3,256,512]{2,1,0:T(8,128)} %get-tuple-element.243.base_ref, bf16[2,256,384]{2,1,0:T(8,128)(2,1)S(1)} %get-tuple-element.244.refs_0_, bf16[2,256,384]{2,1,0:T(8,128)(2,1)S(1)} %collective-permute-done.36.refs_1_, ...), custom_call_target="tpu_custom_call", output_to_operand_aliasing={{}: (0, {})} | custom-call | flops 5500000256 | bytes 1024 | tf_op jit(solution)/shard_map/add_state/pallas_call | solution.py:510
  198.8 1.8 collective-permute-start.47
  200.5 2.2 collective-permute-start.49
  202.7 1.5 collective-permute-done.47.refs_1_
  204.3 2.2 collective-permute-done.49.refs_3_
  207.4 1.5 collective-permute-start.52
  210.1 2.6 %add_state.3 = f32[3,256,512]{2,1,0:T(8,128)} custom-call(f32[3,256,512]{2,1,0:T(8,128)} %add_state.2.base_ref, bf16[1,256,384]{2,1,0:T(8,128)(2,1)S(1)} %get-tuple-element.254.refs_0_, bf16[1,256,384]{2,1,0:T(8,128)(2,1)S(1)} %collective-permute-done.45.refs_1_, ...), custom_call_target="tpu_custom_call", output_to_operand_aliasing={{}: (0, {})} | custom-call | flops 2750000128 | bytes 1024 | tf_op jit(solution)/shard_map/add_state/pallas_call | solution.py:510
  217.0 2.4 %unpack.1 = (f32[512,512]{1,0:T(8,128)}, f32[128,512]{1,0:T(8,128)}, f32[512,512]{1,0:T(8,128)}, f32[8,512]{1,0:T(8,128)S(1)}, f32[512,128]{1,0:T(8,128)}, /*index=5*/f32[512,128]{1,0:T(8,128)}, f32[512,128]{1,0:T(8,128)}) custom-call(s32[3]{0:T(128)S(1)} %pad_add_fusion.info_ref, bf16[200,512]{1,0:T(8,128)(2,1)S(1)} %total.1.refs_0_, ...), custom_call_target="tpu_custom_call" | custom-call | flops 3300000000 | bytes 1024 | tf_op jit(solution)/shard_map/unpack/pallas_call | solution.py:806
  (155 shorter events, 40.9 us)
Async XLA Ops:
  2.5 23.6 %collective-permute-start.2 = (bf16[3,256,512]{2,1,0:T(8,128)(2,1)S(1)}, bf16[3,256,512]{2,1,0:T(8,128)(2,1)S(1)}, u32[]{:S(2)}, u32[]{:S(2)}) collective-permute-start(bf16[3,256,512]{2,1,0:T(8,128)(2,1)S(1)} %get-tuple-element.271.refs_0_), channel_id=1, source_target_pairs={{0,8},{4,12},{8,0},{12,4},{16,24},{20,28},{24,16},{28,20},{1,9},{5... | collective-permute-start | bytes 2359304 | tf_op jit(solution)/shard_map/ppermute | solution.py:1112
  5.5 19.1 %collective-permute-start.3 = (bf16[3,256,512]{2,1,0:T(8,128)(2,1)S(1)}, bf16[3,256,512]{2,1,0:T(8,128)(2,1)}, u32[]{:S(2)}, u32[]{:S(2)}) collective-permute-start(bf16[3,256,512]{2,1,0:T(8,128)(2,1)S(1)} %get-tuple-element.271.refs_0_), channel_id=1, source_target_pairs={{0,16},{4,20},{8,24},{12,28},{16,0},{20,4},{24,8},{28,12},{1,17},{... | collective-permute-start | bytes 2359304 | tf_op jit(solution)/shard_map/ppermute | solution.py:1112
  9.6 8.7 %collective-permute-start.7 = (bf16[256,384]{1,0:T(8,128)(2,1)S(1)}, bf16[256,384]{1,0:T(8,128)(2,1)S(1)}, u32[]{:S(2)}, u32[]{:S(2)}) collective-permute-start(bf16[256,384]{1,0:T(8,128)(2,1)S(1)} %pack.1), channel_id=1, source_target_pairs={{0,1},{4,5},{9,8},{13,12},{18,19},{22,23},{27,26},{31,30}} | collective-permute-start | bytes 589832 | tf_op jit(solution)/shard_map/ppermute | solution.py:1143
  14.6 16.8 %collective-permute-start = (bf16[592,512]{1,0:T(8,128)(2,1)}, bf16[592,512]{1,0:T(8,128)(2,1)}, u32[]{:S(2)}, u32[]{:S(2)}) collective-permute-start(bf16[592,512]{1,0:T(8,128)(2,1)} %pack_feed.1.refs_0_), channel_id=1, source_target_pairs={{0,1},{1,2},{2,3},{3,0},{4,7},{5,4},{6,5},{7,6},{8,9},{9,10},{10,1... | collective-permute-start | bytes 1818632 | tf_op jit(solution)/shard_map/ppermute | solution.py:1135
  14.6 16.8 %collective-permute-start.6 = (bf16[592,512]{1,0:T(8,128)(2,1)}, bf16[592,512]{1,0:T(8,128)(2,1)}, u32[]{:S(2)}, u32[]{:S(2)}) collective-permute-start(bf16[592,512]{1,0:T(8,128)(2,1)} %pack_feed.1.refs_0_), channel_id=1, source_target_pairs={{0,4},{4,0},{8,12},{12,8},{16,20},{20,16},{24,28},{28,24},{1,5},{5... | collective-permute-start | bytes 1818632 | tf_op jit(solution)/shard_map/ppermute | solution.py:1112
  18.4 15.5 %collective-permute-start.8 = (bf16[256,384]{1,0:T(8,128)(2,1)S(1)}, bf16[256,384]{1,0:T(8,128)(2,1)S(1)}, u32[]{:S(2)}, u32[]{:S(2)}) collective-permute-start(bf16[256,384]{1,0:T(8,128)(2,1)S(1)} %broadcast_select_fusion.near_ref), channel_id=1, source_target_pairs={{0,2},{1,3},{4,6},{5,7},{9,11},{8,10},{13,15},{12,14},{18,16},{19,... | collective-permute-start | bytes 589832 | tf_op jit(solution)/shard_map/ppermute | solution.py:1143
  25.7 13.6 %collective-permute-start.4 = (bf16[3,128,512]{2,1,0:T(8,128)(2,1)S(1)}, bf16[3,128,512]{2,1,0:T(8,128)(2,1)S(1)}, u32[]{:S(2)}, u32[]{:S(2)}) collective-permute-start(bf16[3,128,512]{2,1,0:T(8,128)(2,1)S(1)} %slice.66), channel_id=1, source_target_pairs={{0,8},{4,12},{8,0},{12,4},{16,24},{20,28},{24,16},{28,20},{1,9},{5... | collective-permute-start | bytes 1179656 | tf_op jit(solution)/shard_map/ppermute | solution.py:1112
  26.1 13.2 %collective-permute-start.5 = (bf16[3,128,512]{2,1,0:T(8,128)(2,1)S(1)}, bf16[3,128,512]{2,1,0:T(8,128)(2,1)S(1)}, u32[]{:S(2)}, u32[]{:S(2)}) collective-permute-start(bf16[3,128,512]{2,1,0:T(8,128)(2,1)S(1)} %slice.67), channel_id=1, source_target_pairs={{0,16},{4,20},{8,24},{12,28},{16,0},{20,4},{24,8},{28,12},{1,17},{... | collective-permute-start | bytes 1179656 | tf_op jit(solution)/shard_map/ppermute | solution.py:1112
  34.5 21.4 %collective-permute-start.1 = (bf16[592,512]{1,0:T(8,128)(2,1)}, bf16[592,512]{1,0:T(8,128)(2,1)S(1)}, u32[]{:S(2)}, u32[]{:S(2)}) collective-permute-start(bf16[592,512]{1,0:T(8,128)(2,1)} %collective-permute-done.refs_1_), channel_id=1, source_target_pairs={{0,1},{1,2},{2,3},{3,0},{4,7},{5,4},{6,5},{7,6},{8,9},{9,10},{10,1... | collective-permute-start | bytes 1818632 | tf_op jit(solution)/shard_map/ppermute | solution.py:1135
  41.0 6.9 %collective-permute-start.10 = (bf16[1,1024,256]{2,1,0:T(8,128)(2,1)S(1)}, bf16[1,1024,256]{2,1,0:T(8,128)(2,1)S(1)}, u32[]{:S(2)}, u32[]{:S(2)}) collective-permute-start(bf16[1,1024,256]{2,1,0:T(8,128)(2,1)S(1)} %get-tuple-element.148.refs_0_.refs_6_), channel_id=1, source_target_pairs={{0,4},{4,0},{8,12},{12,8},{16,20},{20,16},{24,28},{28,24},{1,5},{5... | collective-permute-start | bytes 1572872 | tf_op jit(solution)/shard_map/ppermute | solution.py:1112
  47.3 8.7 %collective-permute-start.12 = (bf16[1,1024,256]{2,1,0:T(8,128)(2,1)S(1)}, bf16[1,1024,256]{2,1,0:T(8,128)(2,1)S(1)}, u32[]{:S(2)}, u32[]{:S(2)}) collective-permute-start(bf16[1,1024,256]{2,1,0:T(8,128)(2,1)S(1)} %get-tuple-element.154.refs_0_.refs_6_), channel_id=1, source_target_pairs={{0,4},{4,0},{8,12},{12,8},{16,20},{20,16},{24,28},{28,24},{1,5},{5... | collective-permute-start | bytes 1572872 | tf_op jit(solution)/shard_map/ppermute | solution.py:1112
  47.4 8.6 %collective-permute-start.13 = (bf16[1,1024,256]{2,1,0:T(8,128)(2,1)S(1)}, bf16[1,1024,256]{2,1,0:T(8,128)(2,1)S(1)}, u32[]{:S(2)}, u32[]{:S(2)}) collective-permute-start(bf16[1,1024,256]{2,1,0:T(8,128)(2,1)S(1)} %get-tuple-element.156.refs_0_.refs_6_), channel_id=1, source_target_pairs={{0,4},{4,0},{8,12},{12,8},{16,20},{20,16},{24,28},{28,24},{1,5},{5... | collective-permute-start | bytes 1572872 | tf_op jit(solution)/shard_map/ppermute | solution.py:1112
  62.2 17.1 %collective-permute-start.11 = (bf16[592,512]{1,0:T(8,128)(2,1)S(1)}, bf16[592,512]{1,0:T(8,128)(2,1)S(1)}, u32[]{:S(2)}, u32[]{:S(2)}) collective-permute-start(bf16[592,512]{1,0:T(8,128)(2,1)S(1)} %collective-permute-done.1.refs_2_), channel_id=1, source_target_pairs={{0,1},{1,2},{2,3},{3,0},{4,7},{5,4},{6,5},{7,6},{8,9},{9,10},{10,1... | collective-permute-start | bytes 1818632 | tf_op jit(solution)/shard_map/ppermute | solution.py:1135
  70.6 8.8 %collective-permute-start.16 = (bf16[3,256,128]{2,1,0:T(8,128)(2,1)S(1)}, bf16[3,256,128]{2,1,0:T(8,128)(2,1)S(1)}, u32[]{:S(2)}, u32[]{:S(2)}) collective-permute-start(bf16[3,256,128]{2,1,0:T(8,128)(2,1)S(1)} %get-tuple-element.173), channel_id=1, source_target_pairs={{0,8},{4,12},{8,0},{12,4},{16,24},{20,28},{24,16},{28,20},{1,9},{5... | collective-permute-start | bytes 589832 | tf_op jit(solution)/shard_map/ppermute | solution.py:1112
  71.3 11.5 %collective-permute-start.17 = (bf16[3,256,128]{2,1,0:T(8,128)(2,1)S(1)}, bf16[3,256,128]{2,1,0:T(8,128)(2,1)S(1)}, u32[]{:S(2)}, u32[]{:S(2)}) collective-permute-start(bf16[3,256,128]{2,1,0:T(8,128)(2,1)S(1)} %get-tuple-element.174), channel_id=1, source_target_pairs={{0,16},{4,20},{8,24},{12,28},{16,0},{20,4},{24,8},{28,12},{1,17},{... | collective-permute-start | bytes 589832 | tf_op jit(solution)/shard_map/ppermute | solution.py:1112
  71.3 11.5 %collective-permute-start.18 = (bf16[3,256,128]{2,1,0:T(8,128)(2,1)S(1)}, bf16[3,256,128]{2,1,0:T(8,128)(2,1)S(1)}, u32[]{:S(2)}, u32[]{:S(2)}) collective-permute-start(bf16[3,256,128]{2,1,0:T(8,128)(2,1)S(1)} %get-tuple-element.175), channel_id=1, source_target_pairs={{0,24},{4,28},{8,16},{12,20},{16,8},{20,12},{24,0},{28,4},{1,25},{... | collective-permute-start | bytes 589832 | tf_op jit(solution)/shard_map/ppermute | solution.py:1112
  74.1 12.9 %collective-permute-start.15 = (bf16[592,512]{1,0:T(8,128)(2,1)S(1)}, bf16[592,512]{1,0:T(8,128)(2,1)S(1)}, u32[]{:S(2)}, u32[]{:S(2)}) collective-permute-start(bf16[592,512]{1,0:T(8,128)(2,1)S(1)} %collective-permute-done.1.refs_2_), channel_id=1, source_target_pairs={{0,4},{4,0},{8,12},{12,8},{16,20},{20,16},{24,28},{28,24},{1,5},{5... | collective-permute-start | bytes 1818632 | tf_op jit(solution)/shard_map/ppermute | solution.py:1112
  83.5 22.0 %collective-permute-start.23 = (bf16[512,384]{1,0:T(8,128)(2,1)S(1)}, bf16[512,384]{1,0:T(8,128)(2,1)S(1)}, u32[]{:S(2)}, u32[]{:S(2)}) collective-permute-start(bf16[512,384]{1,0:T(8,128)(2,1)S(1)} %assemble.1.refs_5_.refs_4_), channel_id=1, source_target_pairs={{0,8},{4,12},{8,0},{12,4},{16,24},{20,28},{24,16},{28,20},{1,9},{5... | collective-permute-start | bytes 1179656 | tf_op jit(solution)/shard_map/ppermute | solution.py:1112
  84.9 20.5 %collective-permute-start.24 = (bf16[512,384]{1,0:T(8,128)(2,1)S(1)}, bf16[512,384]{1,0:T(8,128)(2,1)S(1)}, u32[]{:S(2)}, u32[]{:S(2)}) collective-permute-start(bf16[512,384]{1,0:T(8,128)(2,1)S(1)} %assemble.1.refs_5_.refs_4_), channel_id=1, source_target_pairs={{0,16},{4,20},{8,24},{12,28},{16,0},{20,4},{24,8},{28,12},{1,17},{... | collective-permute-start | bytes 1179656 | tf_op jit(solution)/shard_map/ppermute | solution.py:1112
  85.3 20.2 %collective-permute-start.25 = (bf16[512,384]{1,0:T(8,128)(2,1)S(1)}, bf16[512,384]{1,0:T(8,128)(2,1)S(1)}, u32[]{:S(2)}, u32[]{:S(2)}) collective-permute-start(bf16[512,384]{1,0:T(8,128)(2,1)S(1)} %assemble.1.refs_5_.refs_4_), channel_id=1, source_target_pairs={{0,24},{4,28},{8,16},{12,20},{16,8},{20,12},{24,0},{28,4},{1,25},{... | collective-permute-start | bytes 1179656 | tf_op jit(solution)/shard_map/ppermute | solution.py:1112
  109.7 7.5 %collective-permute-start.26 = (bf16[4,1,4,80,512]{4,3,2,1,0:T(8,128)(2,1)S(1)}, bf16[4,1,4,80,512]{4,3,2,1,0:T(8,128)(2,1)S(1)}, u32[]{:S(2)}, u32[]{:S(2)}) collective-permute-start(bf16[4,1,4,80,512]{4,3,2,1,0:T(8,128)(2,1)S(1)} %get-tuple-element.200), channel_id=1, source_target_pairs={{0,4},{4,0},{8,12},{12,8},{16,20},{20,16},{24,28},{28,24},{1,5},{5... | collective-permute-start | bytes 3932168 | tf_op jit(solution)/shard_map/ppermute | solution.py:1112
  109.8 9.5 %collective-permute-start.20 = (bf16[3,256,128]{2,1,0:T(8,128)(2,1)S(1)}, bf16[3,256,128]{2,1,0:T(8,128)(2,1)S(1)}, u32[]{:S(2)}, u32[]{:S(2)}) collective-permute-start(bf16[3,256,128]{2,1,0:T(8,128)(2,1)S(1)} %get-tuple-element.183), channel_id=1, source_target_pairs={{0,8},{4,12},{8,0},{12,4},{16,24},{20,28},{24,16},{28,20},{1,9},{5... | collective-permute-start | bytes 589832 | tf_op jit(solution)/shard_map/ppermute | solution.py:1112
  111.3 11.4 %collective-permute-start.21 = (bf16[3,256,128]{2,1,0:T(8,128)(2,1)S(1)}, bf16[3,256,128]{2,1,0:T(8,128)(2,1)S(1)}, u32[]{:S(2)}, u32[]{:S(2)}) collective-permute-start(bf16[3,256,128]{2,1,0:T(8,128)(2,1)S(1)} %get-tuple-element.184), channel_id=1, source_target_pairs={{0,16},{4,20},{8,24},{12,28},{16,0},{20,4},{24,8},{28,12},{1,17},{... | collective-permute-start | bytes 589832 | tf_op jit(solution)/shard_map/ppermute | solution.py:1112
  111.6 11.0 %collective-permute-start.22 = (bf16[3,256,128]{2,1,0:T(8,128)(2,1)S(1)}, bf16[3,256,128]{2,1,0:T(8,128)(2,1)S(1)}, u32[]{:S(2)}, u32[]{:S(2)}) collective-permute-start(bf16[3,256,128]{2,1,0:T(8,128)(2,1)S(1)} %get-tuple-element.185), channel_id=1, source_target_pairs={{0,24},{4,28},{8,16},{12,20},{16,8},{20,12},{24,0},{28,4},{1,25},{... | collective-permute-start | bytes 589832 | tf_op jit(solution)/shard_map/ppermute | solution.py:1112
  117.2 19.3 %collective-permute-start.30 = (bf16[4,1,4,72,512]{4,3,2,1,0:T(8,128)(2,1)S(1)}, bf16[4,1,4,72,512]{4,3,2,1,0:T(8,128)(2,1)S(1)}, u32[]{:S(2)}, u32[]{:S(2)}) collective-permute-start(bf16[4,1,4,72,512]{4,3,2,1,0:T(8,128)(2,1)S(1)} %get-tuple-element.208), channel_id=1, source_target_pairs={{0,4},{4,0},{8,12},{12,8},{16,20},{20,16},{24,28},{28,24},{1,5},{5... | collective-permute-start | bytes 3538952 | tf_op jit(solution)/shard_map/ppermute | solution.py:1112
  117.9 17.6 %collective-permute-start.27 = (bf16[1,4,80,512]{3,2,1,0:T(8,128)(2,1)S(1)}, bf16[1,4,80,512]{3,2,1,0:T(8,128)(2,1)S(1)}, u32[]{:S(2)}, u32[]{:S(2)}) collective-permute-start(bf16[1,4,80,512]{3,2,1,0:T(8,128)(2,1)S(1)} %get-tuple-element.202), channel_id=1, source_target_pairs={{0,8},{4,12},{8,0},{12,4},{16,24},{20,28},{24,16},{28,20},{1,9},{5... | collective-permute-start | bytes 983048 | tf_op jit(solution)/shard_map/ppermute | solution.py:1112
  119.3 17.2 %collective-permute-start.28 = (bf16[1,4,80,512]{3,2,1,0:T(8,128)(2,1)S(1)}, bf16[1,4,80,512]{3,2,1,0:T(8,128)(2,1)S(1)}, u32[]{:S(2)}, u32[]{:S(2)}) collective-permute-start(bf16[1,4,80,512]{3,2,1,0:T(8,128)(2,1)S(1)} %get-tuple-element.203), channel_id=1, source_target_pairs={{0,16},{4,20},{8,24},{12,28},{16,0},{20,4},{24,8},{28,12},{1,17},{... | collective-permute-start | bytes 983048 | tf_op jit(solution)/shard_map/ppermute | solution.py:1112
  122.6 13.9 %collective-permute-start.29 = (bf16[1,4,80,512]{3,2,1,0:T(8,128)(2,1)S(1)}, bf16[1,4,80,512]{3,2,1,0:T(8,128)(2,1)S(1)}, u32[]{:S(2)}, u32[]{:S(2)}) collective-permute-start(bf16[1,4,80,512]{3,2,1,0:T(8,128)(2,1)S(1)} %get-tuple-element.204), channel_id=1, source_target_pairs={{0,24},{4,28},{8,16},{12,20},{16,8},{20,12},{24,0},{28,4},{1,25},{... | collective-permute-start | bytes 983048 | tf_op jit(solution)/shard_map/ppermute | solution.py:1112
  135.4 19.1 %collective-permute-start.34 = (bf16[1,1024,256]{2,1,0:T(8,128)(2,1)S(1)}, bf16[1,1024,256]{2,1,0:T(8,128)(2,1)S(1)}, u32[]{:S(2)}, u32[]{:S(2)}) collective-permute-start(bf16[1,1024,256]{2,1,0:T(8,128)(2,1)S(1)} %get-tuple-element.219), channel_id=1, source_target_pairs={{0,4},{4,0},{8,12},{12,8},{16,20},{20,16},{24,28},{28,24},{1,5},{5... | collective-permute-start | bytes 1572872 | tf_op jit(solution)/shard_map/ppermute | solution.py:1112
  137.0 16.3 %collective-permute-start.31 = (bf16[1,4,72,512]{3,2,1,0:T(8,128)(2,1)S(1)}, bf16[1,4,72,512]{3,2,1,0:T(8,128)(2,1)S(1)}, u32[]{:S(2)}, u32[]{:S(2)}) collective-permute-start(bf16[1,4,72,512]{3,2,1,0:T(8,128)(2,1)S(1)} %get-tuple-element.210), channel_id=1, source_target_pairs={{0,8},{4,12},{8,0},{12,4},{16,24},{20,28},{24,16},{28,20},{1,9},{5... | collective-permute-start | bytes 884744 | tf_op jit(solution)/shard_map/ppermute | solution.py:1112
  137.8 15.6 %collective-permute-start.32 = (bf16[1,4,72,512]{3,2,1,0:T(8,128)(2,1)S(1)}, bf16[1,4,72,512]{3,2,1,0:T(8,128)(2,1)S(1)}, u32[]{:S(2)}, u32[]{:S(2)}) collective-permute-start(bf16[1,4,72,512]{3,2,1,0:T(8,128)(2,1)S(1)} %get-tuple-element.211), channel_id=1, source_target_pairs={{0,16},{4,20},{8,24},{12,28},{16,0},{20,4},{24,8},{28,12},{1,17},{... | collective-permute-start | bytes 884744 | tf_op jit(solution)/shard_map/ppermute | solution.py:1112
  139.6 13.8 %collective-permute-start.33 = (bf16[1,4,72,512]{3,2,1,0:T(8,128)(2,1)S(1)}, bf16[1,4,72,512]{3,2,1,0:T(8,128)(2,1)S(1)}, u32[]{:S(2)}, u32[]{:S(2)}) collective-permute-start(bf16[1,4,72,512]{3,2,1,0:T(8,128)(2,1)S(1)} %get-tuple-element.212), channel_id=1, source_target_pairs={{0,24},{4,28},{8,16},{12,20},{16,8},{20,12},{24,0},{28,4},{1,25},{... | collective-permute-start | bytes 884744 | tf_op jit(solution)/shard_map/ppermute | solution.py:1112
  154.4 25.3 %collective-permute-start.39 = (bf16[2,152,512]{2,1,0:T(8,128)(2,1)S(1)}, bf16[2,152,512]{2,1,0:T(8,128)(2,1)S(1)}, u32[]{:S(2)}, u32[]{:S(2)}) collective-permute-start(bf16[2,152,512]{2,1,0:T(8,128)(2,1)S(1)} %bitcast.35), channel_id=1, source_target_pairs={{0,1},{1,0},{2,3},{3,2},{4,5},{5,4},{6,7},{7,6},{8,9},{9,8},{10,11... | collective-permute-start | bytes 933896 | tf_op jit(solution)/shard_map/ppermute | solution.py:1246
  158.9 16.4 %collective-permute-start.36 = (bf16[2,256,384]{2,1,0:T(8,128)(2,1)S(1)}, bf16[2,256,384]{2,1,0:T(8,128)(2,1)S(1)}, u32[]{:S(2)}, u32[]{:S(2)}) collective-permute-start(bf16[2,256,384]{2,1,0:T(8,128)(2,1)S(1)} %get-tuple-element.226), channel_id=1, source_target_pairs={{0,8},{4,12},{8,0},{12,4},{16,24},{20,28},{24,16},{28,20},{1,9},{5... | collective-permute-start | bytes 1179656 | tf_op jit(solution)/shard_map/ppermute | solution.py:1112
  160.3 18.0 %collective-permute-start.37 = (bf16[2,256,384]{2,1,0:T(8,128)(2,1)S(1)}, bf16[2,256,384]{2,1,0:T(8,128)(2,1)S(1)}, u32[]{:S(2)}, u32[]{:S(2)}) collective-permute-start(bf16[2,256,384]{2,1,0:T(8,128)(2,1)S(1)} %get-tuple-element.227), channel_id=1, source_target_pairs={{0,16},{4,20},{8,24},{12,28},{16,0},{20,4},{24,8},{28,12},{1,17},{... | collective-permute-start | bytes 1179656 | tf_op jit(solution)/shard_map/ppermute | solution.py:1112
  161.5 18.1 %collective-permute-start.38 = (bf16[2,256,384]{2,1,0:T(8,128)(2,1)S(1)}, bf16[2,256,384]{2,1,0:T(8,128)(2,1)S(1)}, u32[]{:S(2)}, u32[]{:S(2)}) collective-permute-start(bf16[2,256,384]{2,1,0:T(8,128)(2,1)S(1)} %get-tuple-element.228), channel_id=1, source_target_pairs={{0,24},{4,28},{8,16},{12,20},{16,8},{20,12},{24,0},{28,4},{1,25},{... | collective-permute-start | bytes 1179656 | tf_op jit(solution)/shard_map/ppermute | solution.py:1112
  185.3 5.9 %collective-permute-start.42 = (bf16[64,384]{1,0:T(8,128)(2,1)S(1)}, bf16[64,384]{1,0:T(8,128)(2,1)S(1)}, u32[]{:S(2)}, u32[]{:S(2)}) collective-permute-start(bf16[64,384]{1,0:T(8,128)(2,1)S(1)} %get-tuple-element.239), channel_id=1, source_target_pairs={{0,8},{4,12},{8,0},{12,4},{16,24},{20,28},{24,16},{28,20},{1,9},{5... | collective-permute-start | bytes 147464 | tf_op jit(solution)/shard_map/ppermute | solution.py:1112
  186.2 4.9 %collective-permute-start.43 = (bf16[64,384]{1,0:T(8,128)(2,1)S(1)}, bf16[64,384]{1,0:T(8,128)(2,1)S(1)}, u32[]{:S(2)}, u32[]{:S(2)}) collective-permute-start(bf16[64,384]{1,0:T(8,128)(2,1)S(1)} %get-tuple-element.240), channel_id=1, source_target_pairs={{0,16},{4,20},{8,24},{12,28},{16,0},{20,4},{24,8},{28,12},{1,17},{... | collective-permute-start | bytes 147464 | tf_op jit(solution)/shard_map/ppermute | solution.py:1112
  187.7 5.5 %collective-permute-start.44 = (bf16[64,384]{1,0:T(8,128)(2,1)S(1)}, bf16[64,384]{1,0:T(8,128)(2,1)S(1)}, u32[]{:S(2)}, u32[]{:S(2)}) collective-permute-start(bf16[64,384]{1,0:T(8,128)(2,1)S(1)} %get-tuple-element.241), channel_id=1, source_target_pairs={{0,24},{4,28},{8,16},{12,20},{16,8},{20,12},{24,0},{28,4},{1,25},{... | collective-permute-start | bytes 147464 | tf_op jit(solution)/shard_map/ppermute | solution.py:1112
  188.8 11.7 %collective-permute-start.45 = (bf16[1,256,384]{2,1,0:T(8,128)(2,1)S(1)}, bf16[1,256,384]{2,1,0:T(8,128)(2,1)S(1)}, u32[]{:S(2)}, u32[]{:S(2)}) collective-permute-start(bf16[1,256,384]{2,1,0:T(8,128)(2,1)S(1)} %get-tuple-element.246), channel_id=1, source_target_pairs={{0,8},{4,12},{8,0},{12,4},{16,24},{20,28},{24,16},{28,20},{1,9},{5... | collective-permute-start | bytes 589832 | tf_op jit(solution)/shard_map/ppermute | solution.py:1112
  189.7 13.0 %collective-permute-start.46 = (bf16[1,256,384]{2,1,0:T(8,128)(2,1)S(1)}, bf16[1,256,384]{2,1,0:T(8,128)(2,1)S(1)}, u32[]{:S(2)}, u32[]{:S(2)}) collective-permute-start(bf16[1,256,384]{2,1,0:T(8,128)(2,1)S(1)} %get-tuple-element.248), channel_id=1, source_target_pairs={{0,16},{4,20},{8,24},{12,28},{16,0},{20,4},{24,8},{28,12},{1,17},{... | collective-permute-start | bytes 589832 | tf_op jit(solution)/shard_map/ppermute | solution.py:1112
  193.8 12.7 %collective-permute-start.48 = (bf16[200,512]{1,0:T(8,128)(2,1)S(1)}, bf16[200,512]{1,0:T(8,128)(2,1)S(1)}, u32[]{:S(2)}, u32[]{:S(2)}) collective-permute-start(bf16[200,512]{1,0:T(8,128)(2,1)S(1)} %get-tuple-element.251), channel_id=1, source_target_pairs={{0,2},{1,3},{2,0},{3,1},{4,6},{5,7},{6,4},{7,5},{8,10},{9,11},{10,... | collective-permute-start | bytes 614408 | tf_op jit(solution)/shard_map/ppermute | solution.py:1246
  197.6 12.5 %collective-permute-start.50 = (bf16[1,256,384]{2,1,0:T(8,128)(2,1)S(1)}, bf16[1,256,384]{2,1,0:T(8,128)(2,1)S(1)}, u32[]{:S(2)}, u32[]{:S(2)}) collective-permute-start(bf16[1,256,384]{2,1,0:T(8,128)(2,1)S(1)} %get-tuple-element.256), channel_id=1, source_target_pairs={{0,24},{4,28},{8,16},{12,20},{16,8},{20,12},{24,0},{28,4},{1,25},{... | collective-permute-start | bytes 589832 | tf_op jit(solution)/shard_map/ppermute | solution.py:1112
  198.8 5.5 %collective-permute-start.47 = (bf16[48,512]{1,0:T(8,128)(2,1)S(1)}, bf16[48,512]{1,0:T(8,128)(2,1)S(1)}, u32[]{:S(2)}, u32[]{:S(2)}) collective-permute-start(bf16[48,512]{1,0:T(8,128)(2,1)S(1)} %get-tuple-element.250), channel_id=1, source_target_pairs={{0,1},{1,0},{2,3},{3,2},{4,5},{5,4},{6,7},{7,6},{8,9},{9,8},{10,11... | collective-permute-start | bytes 147464 | tf_op jit(solution)/shard_map/ppermute | solution.py:1246
  200.5 5.9 %collective-permute-start.49 = (bf16[48,512]{1,0:T(8,128)(2,1)S(1)}, bf16[48,512]{1,0:T(8,128)(2,1)S(1)}, u32[]{:S(2)}, u32[]{:S(2)}) collective-permute-start(bf16[48,512]{1,0:T(8,128)(2,1)S(1)} %get-tuple-element.252), channel_id=1, source_target_pairs={{0,3},{1,2},{2,1},{3,0},{4,7},{5,6},{6,5},{7,4},{8,11},{9,10},{10,... | collective-permute-start | bytes 147464 | tf_op jit(solution)/shard_map/ppermute | solution.py:1246
  206.5 6.2 %collective-permute-start.51 = (bf16[200,512]{1,0:T(8,128)(2,1)S(1)}, bf16[200,512]{1,0:T(8,128)(2,1)S(1)}, u32[]{:S(2)}, u32[]{:S(2)}) collective-permute-start(bf16[200,512]{1,0:T(8,128)(2,1)S(1)} %total.1.refs_0_), channel_id=1, source_target_pairs={{0,8},{4,12},{8,0},{12,4},{16,24},{20,28},{24,16},{28,20},{1,9},{5... | collective-permute-start | bytes 614408 | tf_op jit(solution)/shard_map/ppermute | solution.py:1112
  207.4 7.0 %collective-permute-start.52 = (bf16[200,512]{1,0:T(8,128)(2,1)S(1)}, bf16[200,512]{1,0:T(8,128)(2,1)S(1)}, u32[]{:S(2)}, u32[]{:S(2)}) collective-permute-start(bf16[200,512]{1,0:T(8,128)(2,1)S(1)} %total.1.refs_0_), channel_id=1, source_target_pairs={{0,16},{4,20},{8,24},{12,28},{16,0},{20,4},{24,8},{28,12},{1,17},{... | collective-permute-start | bytes 614408 | tf_op jit(solution)/shard_map/ppermute | solution.py:1112
  208.9 6.7 %collective-permute-start.53 = (bf16[200,512]{1,0:T(8,128)(2,1)S(1)}, bf16[200,512]{1,0:T(8,128)(2,1)S(1)}, u32[]{:S(2)}, u32[]{:S(2)}) collective-permute-start(bf16[200,512]{1,0:T(8,128)(2,1)S(1)} %total.1.refs_0_), channel_id=1, source_target_pairs={{0,24},{4,28},{8,16},{12,20},{16,8},{20,12},{24,0},{28,4},{1,25},{... | collective-permute-start | bytes 614408 | tf_op jit(solution)/shard_map/ppermute | solution.py:1112
  (31 other events, 218.8 us)
